TPU v7x, 128 devices: a whole 4x4x4 slice. The times are simulated.
128 devices in a mesh: section: 2 (over x_lo), fsdp: 4 (over x_hi, core), tensor: 16 (over y, z).
Axes of the slice: x: 4 (x_hi: 2, x_lo: 2; x = x_hi * 2 + x_lo), y: 4, z: 4, core: 2. Of those that a mesh axis runs over, the one named last changes fastest.
Arguments:
- ends_in: bfloat16 [2, 4, 4, 1024, 1152], P('section', None, 'fsdp', 'tensor'), may hold values from -6 to 6
- w_qkv: bfloat16 [2, 1152, 3, 1152], P('section', 'fsdp', None, 'tensor'), may hold values from -0.1875 to 0.1875
- b_qv: float32 [2, 2, 1152], P('section', None, 'tensor'), may hold values from -0.6 to 0.6
- w_out: bfloat16 [2, 1152, 1152], P('section', 'tensor', 'fsdp'), may hold values from -1.5 to 1.5
- w_up: bfloat16 [2, 1152, 4304], P('section', 'fsdp', 'tensor'), may hold values from -0.1875 to 0.1875
- b_up: float32 [2, 4304], P('section', 'tensor'), may hold values from -3 to 3
- w_down: bfloat16 [2, 4304, 1152], P('section', 'tensor', 'fsdp'), may hold values from -0.09375 to 0.09375
- gains: float32 [2, 2, 1152], P('section', None, ('fsdp', 'tensor')), may hold values from 0.1 to 1.9
- shifts: float32 [2, 4, 1152], P('section', None, ('fsdp', 'tensor')), may hold values from -1.8 to 1.8
Outputs:
- ends_out: bfloat16 [2, 4, 4, 1024, 1152], P('section', None, 'fsdp', 'tensor')
- grad_w_qkv: float32 [2, 1152, 3, 1152], P('section', 'fsdp', None, 'tensor')
- grad_b_qv: float32 [2, 2, 1152], P('section', None, 'tensor')
- grad_w_out: float32 [2, 1152, 1152], P('section', 'tensor', 'fsdp')
- grad_w_up: float32 [2, 1152, 4304], P('section', 'fsdp', 'tensor')
- grad_b_up: float32 [2, 4304], P('section', 'tensor')
- grad_w_down: float32 [2, 4304, 1152], P('section', 'tensor', 'fsdp')
- grad_gains: float32 [2, 2, 1152], P('section', None, ('fsdp', 'tensor'))
- grad_shifts: float32 [2, 4, 1152], P('section', None, ('fsdp', 'tensor'))
All inputs are finite; a program needn't handle non-finite values.
Results may differ from a plain program's by a relative error of at most 0.017.
Values may be sent and summed in bfloat16 or wider, within the bound.
No kernel may reach another device: no remote copies, remote signals or barrier semaphores. Data moves between devices by JAX's collectives and lax.ppermute only.
A program may use at most 256 MiB of HBM per device.

v0:
```python
from functools import partial

import jax
import jax.numpy as jnp
from jax import lax
from jax.sharding import PartitionSpec as P

HD = 72


norm_epsilon = 1e-06


def shifted(block, axis, distance):
    devices = range(lax.axis_size(axis))
    route = [(i - distance, i) for i in devices if i - distance in devices]
    return lax.ppermute(block, axis, route)


def norm_rows(hidden, gain_row, offset_row):
    average = jnp.mean(hidden, axis=-1, keepdims=True)
    centered = hidden - average
    inv_spread = lax.rsqrt(jnp.mean(centered * centered, axis=-1, keepdims=True) + norm_epsilon)
    normed = centered * inv_spread
    return (normed * gain_row + offset_row, normed, inv_spread)


def norm_back(carried, grad_normed, normed, inv_spread, gain_row):
    scaled = grad_normed * gain_row
    inner_mean = jnp.mean(scaled, axis=-1, keepdims=True)
    cross_mean = jnp.mean(scaled * normed, axis=-1, keepdims=True)
    grad_hidden = carried + inv_spread * (scaled - inner_mean - normed * cross_mean)
    return (
        grad_hidden,
        jnp.sum(grad_normed * normed, axis=(0, 1)),
        jnp.sum(grad_normed, axis=(0, 1)),
    )


def gelu_tanh(values):
    return jax.nn.gelu(values, approximate=True)


def split_heads(merged):
    return merged.reshape(merged.shape[0], merged.shape[1], merged.shape[2] // HD, HD)


def spread_rows(rows_low):
    return lax.all_gather(rows_low, "tensor", axis=1, tiled=True)


def collect_rows(summand):
    return lax.psum_scatter(
        summand.astype(jnp.bfloat16), "tensor", scatter_dimension=1, tiled=True
    ).astype(jnp.float32)


def fetch_weights(w_qkv, w_out, w_up, w_down):
    rows_qkv, rows_out, rows_up, rows_down = (
        lax.all_gather(w_qkv, "fsdp", axis=1, tiled=True),
        lax.all_gather(w_out, "fsdp", axis=2, tiled=True),
        lax.all_gather(w_up, "fsdp", axis=1, tiled=True),
        lax.all_gather(w_down, "fsdp", axis=2, tiled=True),
    )
    full_out = rows_out[0]
    return (rows_qkv[0], full_out, rows_up[0], rows_down[0])


def forward_layer(hidden, weights, biases, vectors):
    w_qkv, w_out, w_up, w_down = weights
    b_qv, b_up = biases
    gains, shifts = vectors
    normed_first, unit_first, scale_first = norm_rows(hidden, gains[0], shifts[0])
    rows_first = spread_rows(normed_first.astype(jnp.bfloat16))
    projected = jnp.einsum("isd,dcf->cisf", rows_first, w_qkv, preferred_element_type=jnp.float32)
    query_heads = split_heads((projected[0] + b_qv[0]).astype(jnp.bfloat16))
    key_heads = split_heads(projected[1].astype(jnp.bfloat16))
    value_heads = split_heads((projected[2] + b_qv[1]).astype(jnp.bfloat16))
    scores = jnp.einsum(
        "iqhe,ikhe->ihqk", query_heads, key_heads, preferred_element_type=jnp.float32
    ) * HD ** (-0.5)
    row_max = jnp.max(scores, axis=-1, keepdims=True)
    raised = jnp.exp(scores - row_max)
    row_sum = jnp.sum(raised, axis=-1, keepdims=True)
    attention = (raised / row_sum).astype(jnp.bfloat16)
    log_total = (row_max + jnp.log(row_sum))[..., 0]
    mixed_heads = jnp.einsum(
        "ihqk,ikhe->iqhe", attention, value_heads, preferred_element_type=jnp.float32
    )
    attended = mixed_heads.astype(jnp.bfloat16).reshape(
        rows_first.shape[0], rows_first.shape[1], -1
    )
    branch = collect_rows(
        jnp.einsum("isf,fd->isd", attended, w_out, preferred_element_type=jnp.float32)
    )
    middle = hidden + (branch + shifts[1])
    normed_second, unit_second, scale_second = norm_rows(middle, gains[1], shifts[2])
    rows_second = spread_rows(normed_second.astype(jnp.bfloat16))
    pre_act = (
        jnp.einsum("isd,df->isf", rows_second, w_up, preferred_element_type=jnp.float32) + b_up
    )
    activated = gelu_tanh(pre_act).astype(jnp.bfloat16)
    mlp_out = collect_rows(
        jnp.einsum("isf,fd->isd", activated, w_down, preferred_element_type=jnp.float32)
    )
    result = middle + (mlp_out + shifts[3])
    stored = (
        unit_first,
        scale_first,
        rows_first,
        query_heads,
        key_heads,
        value_heads,
        log_total,
        attended,
        unit_second,
        scale_second,
        rows_second,
        pre_act,
        activated,
    )
    return (result, stored)


def backward_layer(grad_out, stored, weights, vectors):
    (
        unit_first,
        scale_first,
        rows_first,
        query_heads,
        key_heads,
        value_heads,
        log_total,
        out_input,
        unit_second,
        scale_second,
        rows_second,
        pre_act,
        activated,
    ) = stored
    w_qkv, w_out, w_up, w_down = weights
    gains, shifts = vectors
    down_rows = spread_rows(grad_out.astype(jnp.bfloat16))
    grad_w_down = jnp.einsum(
        "isf,isd->fd", activated, down_rows, preferred_element_type=jnp.float32
    )
    grad_act = jnp.einsum("isd,fd->isf", down_rows, w_down, preferred_element_type=jnp.float32)
    gelu_pull = jax.vjp(gelu_tanh, pre_act)[1]
    grad_pre = gelu_pull(grad_act)[0]
    pre_low = grad_pre.astype(jnp.bfloat16)
    grad_w_up = jnp.einsum("isd,isf->df", rows_second, pre_low, preferred_element_type=jnp.float32)
    grad_rows_second = collect_rows(
        jnp.einsum("isf,df->isd", pre_low, w_up, preferred_element_type=jnp.float32)
    )
    grad_middle, gain_second, offset_second = norm_back(
        grad_out, grad_rows_second, unit_second, scale_second, gains[1]
    )
    middle_low = grad_middle.astype(jnp.bfloat16)
    out_rows = spread_rows(middle_low)
    grad_w_out = jnp.einsum("isf,isd->fd", out_input, out_rows, preferred_element_type=jnp.float32)
    grad_attended = jnp.einsum(
        "isd,fd->isf", out_rows, w_out, preferred_element_type=jnp.float32
    ).astype(jnp.bfloat16)
    grad_heads = split_heads(grad_attended)
    scores = jnp.einsum(
        "iqhe,ikhe->ihqk", query_heads, key_heads, preferred_element_type=jnp.float32
    ) * HD ** (-0.5)
    attention = jnp.exp(scores - log_total[..., None])
    grad_value = jnp.einsum(
        "ihqk,iqhe->ikhe",
        attention.astype(jnp.bfloat16),
        grad_heads,
        preferred_element_type=jnp.float32,
    )
    grad_attention = jnp.einsum(
        "iqhe,ikhe->ihqk", grad_heads, value_heads, preferred_element_type=jnp.float32
    )
    grad_scores = (
        attention * (grad_attention - jnp.sum(attention * grad_attention, axis=-1, keepdims=True))
    ).astype(jnp.bfloat16)
    grad_query = jnp.einsum(
        "ihqk,ikhe->iqhe", grad_scores, key_heads, preferred_element_type=jnp.float32
    ) * HD ** (-0.5)
    grad_key = jnp.einsum(
        "ihqk,iqhe->ikhe", grad_scores, query_heads, preferred_element_type=jnp.float32
    ) * HD ** (-0.5)
    stacked = jnp.stack([grad_query, grad_key, grad_value]).reshape(
        3, rows_first.shape[0], rows_first.shape[1], -1
    )
    grad_b_qv = jnp.sum(stacked[0::2], axis=(1, 2))
    stacked_low = stacked.astype(jnp.bfloat16)
    grad_w_qkv = jnp.einsum(
        "isd,cisf->dcf", rows_first, stacked_low, preferred_element_type=jnp.float32
    )
    grad_rows_first = collect_rows(
        jnp.einsum("cisf,dcf->isd", stacked_low, w_qkv, preferred_element_type=jnp.float32)
    )
    grad_hidden, gain_first, offset_first = norm_back(
        grad_middle, grad_rows_first, unit_first, scale_first, gains[0]
    )
    grad_gains = jnp.stack([gain_first, gain_second])
    grad_shifts = jnp.stack(
        [
            offset_first,
            jnp.sum(grad_middle, axis=(0, 1)),
            offset_second,
            jnp.sum(grad_out, axis=(0, 1)),
        ]
    )
    return (
        grad_hidden,
        (grad_w_qkv, grad_w_out, grad_w_up, grad_w_down),
        (grad_b_qv, jnp.sum(grad_pre, axis=(0, 1))),
        (grad_gains, grad_shifts),
    )


def pick_leaf(choose_first, first_leaf, second_leaf):
    return jnp.where(choose_first, first_leaf, second_leaf)


def add_tuples(running, extra):
    if running is None:
        return extra
    return tuple((left + right for left, right in zip(running, extra)))


def body(ends_in, w_qkv, b_qv, w_out, w_up, b_up, w_down, gains, shifts):
    is_first = lax.axis_index("section") == 0
    local_in = ends_in[0]
    micro_count = local_in.shape[0]
    moments = micro_count + 1
    gains_full, shifts_full = (
        lax.all_gather(gains, ("fsdp", "tensor"), axis=2, tiled=True),
        lax.all_gather(shifts, ("fsdp", "tensor"), axis=2, tiled=True),
    )
    vectors = (gains_full[0], shifts_full[0])
    biases = (b_qv[0], b_up[0])
    received = jnp.zeros(local_in.shape[1:], jnp.bfloat16)
    outputs = []
    stored_list = []
    for moment in range(moments):
        weights = fetch_weights(w_qkv, w_out, w_up, w_down)
        fresh_input = local_in[min(moment, micro_count - 1)]
        hidden = jnp.where(is_first, fresh_input, received).astype(jnp.float32)
        result, stored = forward_layer(hidden, weights, biases, vectors)
        outgoing = result.astype(jnp.bfloat16)
        outputs.append(outgoing)
        stored_list.append(stored)
        if moment + 1 < moments:
            received = shifted(outgoing, "section", 1)
    arriving = jnp.zeros(local_in.shape[1:], jnp.bfloat16)
    input_grads = []
    weight_totals = None
    bias_totals = None
    vector_totals = None
    for moment in range(moments):
        weights = fetch_weights(w_qkv, w_out, w_up, w_down)
        if moment < micro_count:
            own_grad = local_in[moment]
        else:
            own_grad = jnp.zeros_like(arriving)
        grad_out = jnp.where(is_first, arriving, own_grad).astype(jnp.float32)
        earlier = stored_list[max(moment - 1, 0)]
        later_store = stored_list[min(moment + 1, micro_count)]
        stored = jax.tree.map(partial(pick_leaf, is_first), earlier, later_store)
        grad_hidden, weight_parts, bias_parts, vector_parts = backward_layer(
            grad_out, stored, weights, vectors
        )
        grad_sent = grad_hidden.astype(jnp.bfloat16)
        input_grads.append(grad_sent)
        if moment + 1 < moments:
            arriving = shifted(grad_sent, "section", -1)
        weight_totals = add_tuples(weight_totals, weight_parts)
        bias_totals = add_tuples(bias_totals, bias_parts)
        vector_totals = add_tuples(vector_totals, vector_parts)
    total_qkv, total_out, total_up, total_down = weight_totals
    share_qkv, share_out, share_up, share_down = (
        lax.psum_scatter(
            total_qkv.astype(jnp.bfloat16), "fsdp", scatter_dimension=0, tiled=True
        ).astype(jnp.float32),
        lax.psum_scatter(
            total_out.astype(jnp.bfloat16), "fsdp", scatter_dimension=1, tiled=True
        ).astype(jnp.float32),
        lax.psum_scatter(
            total_up.astype(jnp.bfloat16), "fsdp", scatter_dimension=0, tiled=True
        ).astype(jnp.float32),
        lax.psum_scatter(
            total_down.astype(jnp.bfloat16), "fsdp", scatter_dimension=1, tiled=True
        ).astype(jnp.float32),
    )
    bias_qv, bias_up = lax.psum((bias_totals[0], bias_totals[1]), "fsdp")
    gain_share, shift_share = (
        lax.psum_scatter(vector_totals[0], ("fsdp", "tensor"), scatter_dimension=1, tiled=True),
        lax.psum_scatter(vector_totals[1], ("fsdp", "tensor"), scatter_dimension=1, tiled=True),
    )
    ends_out = jnp.where(is_first, jnp.stack(input_grads[1:]), jnp.stack(outputs[1:]))[None]
    return (
        ends_out,
        share_qkv[None],
        bias_qv[None],
        share_out[None],
        share_up[None],
        bias_up[None],
        share_down[None],
        gain_share[None],
        shift_share[None],
    )


def solution(mesh):
    return jax.shard_map(
        body,
        mesh=mesh,
        in_specs=(
            P("section", None, "fsdp", "tensor", None),
            P("section", "fsdp", None, "tensor"),
            P("section", None, "tensor"),
            P("section", "tensor", "fsdp"),
            P("section", "fsdp", "tensor"),
            P("section", "tensor"),
            P("section", "tensor", "fsdp"),
            P("section", None, ("fsdp", "tensor")),
            P("section", None, ("fsdp", "tensor")),
        ),
        out_specs=(
            P("section", None, "fsdp", "tensor", None),
            P("section", "fsdp", None, "tensor"),
            P("section", None, "tensor"),
            P("section", "tensor", "fsdp"),
            P("section", "fsdp", "tensor"),
            P("section", "tensor"),
            P("section", "tensor", "fsdp"),
            P("section", None, ("fsdp", "tensor")),
            P("section", None, ("fsdp", "tensor")),
        ),
        check_vma=False,
    )
```

profile of v0, /device:TPU:0, one launch (start us, length us, event | category | flops | bytes accessed | tf_op | source)
XLA Modules:
  0.0 3476.9 jit_solution(11772443218394635460)
XLA Ops:
  12.1 171.6 %all_gather.53 = f32[1,4,1152]{1,0,2:T(1,128)S(1)} all-gather(f32[1,4,18]{1,0,2:T(1,128)S(1)} %copy.30), channel_id=1, replica_groups=mesh['section'=2,'fsdp'=4,'tensor'=16] {'fsdp','tensor'}, dimensions={2}, use_global_device_ids=true | all-gather | bytes 18720 | tf_op jit(solution)/shard_map/all_gather | solution.py:235
  183.7 24.4 slice_reduce_fusion
  208.1 163.3 %all_gather.52 = f32[1,2,1152]{1,0,2:T(1,128)S(1)} all-gather(f32[1,2,18]{1,0,2:T(1,128)S(1)} %copy.29), channel_id=1, replica_groups=mesh['section'=2,'fsdp'=4,'tensor'=16] {'fsdp','tensor'}, dimensions={2}, use_global_device_ids=true | all-gather | bytes 9360 | tf_op jit(solution)/shard_map/all_gather | solution.py:234
  371.4 18.6 slice_reduce_fusion.5
  391.3 8.2 all_gather.56
  400.1 12.4 all_gather.55
  413.2 19.8 all-gather.22.cloned.1.call-done
  441.0 74.0 %reduce-scatter.35.cloned.1.call-done = bf16[1,64,1152]{2,1,0:T(8,128)(2,1)} async-done(((bf16[1,1024,1152]{2,1,0:T(8,128)(2,1)}), bf16[1,64,1152]{2,1,0:T(8,128)(2,1)}) %reduce-scatter.35.cloned.1.call-update) | async-done | bytes 147472 | tf_op jit(solution)/shard_map/reduce_scatter | solution.py:53
  520.7 15.9 all_gather.59
  536.6 4.4 copy.38
  541.1 16.2 all_gather.58
  557.2 4.4 copy.36
  570.9 74.4 %reduce-scatter.37.cloned.1.call-done = bf16[1,64,1152]{2,1,0:T(8,128)(2,1)} async-done(((bf16[1,1024,1152]{2,1,0:T(8,128)(2,1)}), bf16[1,64,1152]{2,1,0:T(8,128)(2,1)}) %reduce-scatter.37.cloned.1.call-update) | async-done | bytes 147472 | tf_op jit(solution)/shard_map/reduce_scatter | solution.py:53
  654.1 45.8 %all-gather.26.cloned.1.call-done = bf16[1,1024,1152]{2,1,0:T(8,128)(2,1)} async-done(((bf16[1,64,1152]{2,1,0:T(8,128)(2,1)}), bf16[1,1024,1152]{2,1,0:T(8,128)(2,1)}) %all-gather.26.cloned.1.call-update) | async-done | bytes 2359312 | tf_op jit(solution)/shard_map/all_gather | solution.py:49
  707.4 74.4 %reduce-scatter.39.cloned.1.call-done = bf16[1,64,1152]{2,1,0:T(8,128)(2,1)} async-done(((bf16[1,1024,1152]{2,1,0:T(8,128)(2,1)}), bf16[1,64,1152]{2,1,0:T(8,128)(2,1)}) %reduce-scatter.39.cloned.1.call-update) | async-done | bytes 147472 | tf_op jit(solution)/shard_map/reduce_scatter | solution.py:53
  787.3 44.1 %all-gather.28.cloned.1.call-done = bf16[1,1024,1152]{2,1,0:T(8,128)(2,1)} async-done(((bf16[1,64,1152]{2,1,0:T(8,128)(2,1)}), bf16[1,1024,1152]{2,1,0:T(8,128)(2,1)}) %all-gather.28.cloned.1.call-update) | async-done | bytes 2359312 | tf_op jit(solution)/shard_map/all_gather | solution.py:49
  839.3 39.9 %all-gather.60.cloned.1.call-done = bf16[1,1,1,1024,1152]{4,3,2,1,0:T(8,128)(2,1)} async-done(((bf16[1,1,1,64,1152]{4,3,2,1,0:T(8,128)(2,1)}), bf16[1,1,1,1024,1152]{4,3,2,1,0:T(8,128)(2,1)}) %all-gather.60.cloned.1.call-update) | async-done | bytes 2359312 | tf_op jit(solution)/shard_map/all_gather | solution.py:49
  888.4 68.5 %reduce-scatter.45.cloned.1.call-done = bf16[1,64,1152]{2,1,0:T(8,128)(2,1)} async-done(((bf16[1,1024,1152]{2,1,0:T(8,128)(2,1)}), bf16[1,64,1152]{2,1,0:T(8,128)(2,1)}) %reduce-scatter.45.cloned.1.call-update) | async-done | bytes 147472 | tf_op jit(solution)/shard_map/reduce_scatter | solution.py:53
  961.3 73.0 %reduce-scatter.41.cloned.1.call-done = bf16[1,64,1152]{2,1,0:T(8,128)(2,1)} async-done(((bf16[1,1024,1152]{2,1,0:T(8,128)(2,1)}), bf16[1,64,1152]{2,1,0:T(8,128)(2,1)}) %reduce-scatter.41.cloned.1.call-update) | async-done | bytes 147472 | tf_op jit(solution)/shard_map/reduce_scatter | solution.py:53
  1037.9 45.0 %all-gather.32.cloned.1.call-done = bf16[1,1024,1152]{2,1,0:T(8,128)(2,1)} async-done(((bf16[1,64,1152]{2,1,0:T(8,128)(2,1)}), bf16[1,1024,1152]{2,1,0:T(8,128)(2,1)}) %all-gather.32.cloned.1.call-update) | async-done | bytes 2359312 | tf_op jit(solution)/shard_map/all_gather | solution.py:49
  1090.6 74.5 %reduce-scatter.47.cloned.1.call-done = bf16[1,64,1152]{2,1,0:T(8,128)(2,1)} async-done(((bf16[1,1024,1152]{2,1,0:T(8,128)(2,1)}), bf16[1,64,1152]{2,1,0:T(8,128)(2,1)}) %reduce-scatter.47.cloned.1.call-update) | async-done | bytes 147472 | tf_op jit(solution)/shard_map/reduce_scatter | solution.py:53
  1171.0 44.1 %all-gather.36.cloned.1.call-done = bf16[1,1024,1152]{2,1,0:T(8,128)(2,1)} async-done(((bf16[1,64,1152]{2,1,0:T(8,128)(2,1)}), bf16[1,1024,1152]{2,1,0:T(8,128)(2,1)}) %all-gather.36.cloned.1.call-update) | async-done | bytes 2359312 | tf_op jit(solution)/shard_map/all_gather | solution.py:49
  1225.9 37.0 %all-gather.30.cloned.1.call-done = bf16[1,1024,1152]{2,1,0:T(8,128)(2,1)} async-done(((bf16[1,64,1152]{2,1,0:T(8,128)(2,1)}), bf16[1,1024,1152]{2,1,0:T(8,128)(2,1)}) %all-gather.30.cloned.1.call-update) | async-done | bytes 2359312 | tf_op jit(solution)/shard_map/all_gather | solution.py:49
  1275.9 64.5 %reduce-scatter.53.cloned.1.call-done = bf16[1,64,1152]{2,1,0:T(8,128)(2,1)} async-done(((bf16[1,1024,1152]{2,1,0:T(8,128)(2,1)}), bf16[1,64,1152]{2,1,0:T(8,128)(2,1)}) %reduce-scatter.53.cloned.1.call-update) | async-done | bytes 147472 | tf_op jit(solution)/shard_map/reduce_scatter | solution.py:53
  1344.8 73.0 %reduce-scatter.43.cloned.1.call-done = bf16[1,64,1152]{2,1,0:T(8,128)(2,1)} async-done(((bf16[1,1024,1152]{2,1,0:T(8,128)(2,1)}), bf16[1,64,1152]{2,1,0:T(8,128)(2,1)}) %reduce-scatter.43.cloned.1.call-update) | async-done | bytes 147472 | tf_op jit(solution)/shard_map/reduce_scatter | solution.py:53
  1421.2 44.7 %all-gather.40.cloned.1.call-done = bf16[1,1024,1152]{2,1,0:T(8,128)(2,1)} async-done(((bf16[1,64,1152]{2,1,0:T(8,128)(2,1)}), bf16[1,1024,1152]{2,1,0:T(8,128)(2,1)}) %all-gather.40.cloned.1.call-update) | async-done | bytes 2359312 | tf_op jit(solution)/shard_map/all_gather | solution.py:49
  1473.4 74.5 %reduce-scatter.55.cloned.1.call-done = bf16[1,64,1152]{2,1,0:T(8,128)(2,1)} async-done(((bf16[1,1024,1152]{2,1,0:T(8,128)(2,1)}), bf16[1,64,1152]{2,1,0:T(8,128)(2,1)}) %reduce-scatter.55.cloned.1.call-update) | async-done | bytes 147472 | tf_op jit(solution)/shard_map/reduce_scatter | solution.py:53
  1551.9 45.1 %all-gather.44.cloned.1.call-done = bf16[1,1024,1152]{2,1,0:T(8,128)(2,1)} async-done(((bf16[1,64,1152]{2,1,0:T(8,128)(2,1)}), bf16[1,1024,1152]{2,1,0:T(8,128)(2,1)}) %all-gather.44.cloned.1.call-update) | async-done | bytes 2359312 | tf_op jit(solution)/shard_map/all_gather | solution.py:49
  1605.0 73.3 %reduce-scatter.61.cloned.1.call-done = bf16[1,64,1152]{2,1,0:T(8,128)(2,1)} async-done(((bf16[1,1024,1152]{2,1,0:T(8,128)(2,1)}), bf16[1,64,1152]{2,1,0:T(8,128)(2,1)}) %reduce-scatter.61.cloned.1.call-update) | async-done | bytes 147472 | tf_op jit(solution)/shard_map/reduce_scatter | solution.py:53
  1691.7 5.9 collective-permute-done.1
  1699.0 37.1 %all-gather.48.cloned.1.call-done = bf16[1,1024,1152]{2,1,0:T(8,128)(2,1)} async-done(((bf16[1,64,1152]{2,1,0:T(8,128)(2,1)}), bf16[1,1024,1152]{2,1,0:T(8,128)(2,1)}) %all-gather.48.cloned.1.call-update) | async-done | bytes 2359312 | tf_op jit(solution)/shard_map/all_gather | solution.py:49
  1744.6 39.4 %all-gather.34.cloned.1.call-done = bf16[1,1024,1152]{2,1,0:T(8,128)(2,1)} async-done(((bf16[1,64,1152]{2,1,0:T(8,128)(2,1)}), bf16[1,1024,1152]{2,1,0:T(8,128)(2,1)}) %all-gather.34.cloned.1.call-update) | async-done | bytes 2359312 | tf_op jit(solution)/shard_map/all_gather | solution.py:49
  1784.0 4.3 fusion.598
  1792.2 69.5 %reduce-scatter.63.cloned.1.call-done = bf16[1,64,1152]{2,1,0:T(8,128)(2,1)} async-done(((bf16[1,1024,1152]{2,1,0:T(8,128)(2,1)}), bf16[1,64,1152]{2,1,0:T(8,128)(2,1)}) %reduce-scatter.63.cloned.1.call-update) | async-done | bytes 147472 | tf_op jit(solution)/shard_map/reduce_scatter | solution.py:53
  1865.1 73.9 %reduce-scatter.49.cloned.1.call-done = bf16[1,64,1152]{2,1,0:T(8,128)(2,1)} async-done(((bf16[1,1024,1152]{2,1,0:T(8,128)(2,1)}), bf16[1,64,1152]{2,1,0:T(8,128)(2,1)}) %reduce-scatter.49.cloned.1.call-update) | async-done | bytes 147472 | tf_op jit(solution)/shard_map/reduce_scatter | solution.py:53
  1948.3 41.1 %all-gather.38.cloned.1.call-done = bf16[1,1024,1152]{2,1,0:T(8,128)(2,1)} async-done(((bf16[1,64,1152]{2,1,0:T(8,128)(2,1)}), bf16[1,1024,1152]{2,1,0:T(8,128)(2,1)}) %all-gather.38.cloned.1.call-update) | async-done | bytes 2359312 | tf_op jit(solution)/shard_map/all_gather | solution.py:49
  2004.5 74.4 %reduce-scatter.51.cloned.1.call-done = bf16[1,64,1152]{2,1,0:T(8,128)(2,1)} async-done(((bf16[1,1024,1152]{2,1,0:T(8,128)(2,1)}), bf16[1,64,1152]{2,1,0:T(8,128)(2,1)}) %reduce-scatter.51.cloned.1.call-update) | async-done | bytes 147472 | tf_op jit(solution)/shard_map/reduce_scatter | solution.py:53
  2083.5 5.7 collective-permute-done.3
  2090.2 44.8 %all-gather.42.cloned.1.call-done = bf16[1,1024,1152]{2,1,0:T(8,128)(2,1)} async-done(((bf16[1,64,1152]{2,1,0:T(8,128)(2,1)}), bf16[1,1024,1152]{2,1,0:T(8,128)(2,1)}) %all-gather.42.cloned.1.call-update) | async-done | bytes 2359312 | tf_op jit(solution)/shard_map/all_gather | solution.py:49
  2135.1 4.3 fusion.596
  2143.2 74.4 %reduce-scatter.57.cloned.1.call-done = bf16[1,64,1152]{2,1,0:T(8,128)(2,1)} async-done(((bf16[1,1024,1152]{2,1,0:T(8,128)(2,1)}), bf16[1,64,1152]{2,1,0:T(8,128)(2,1)}) %reduce-scatter.57.cloned.1.call-update) | async-done | bytes 147472 | tf_op jit(solution)/shard_map/reduce_scatter | solution.py:53
  2226.4 41.3 %all-gather.46.cloned.1.call-done = bf16[1,1024,1152]{2,1,0:T(8,128)(2,1)} async-done(((bf16[1,64,1152]{2,1,0:T(8,128)(2,1)}), bf16[1,1024,1152]{2,1,0:T(8,128)(2,1)}) %all-gather.46.cloned.1.call-update) | async-done | bytes 2359312 | tf_op jit(solution)/shard_map/all_gather | solution.py:49
  2283.5 73.7 %reduce-scatter.59.cloned.1.call-done = bf16[1,64,1152]{2,1,0:T(8,128)(2,1)} async-done(((bf16[1,1024,1152]{2,1,0:T(8,128)(2,1)}), bf16[1,64,1152]{2,1,0:T(8,128)(2,1)}) %reduce-scatter.59.cloned.1.call-update) | async-done | bytes 147472 | tf_op jit(solution)/shard_map/reduce_scatter | solution.py:53
  2361.6 5.7 collective-permute-done.5
  2369.1 35.8 %all-gather.52.cloned.1.call-done = bf16[1,1024,1152]{2,1,0:T(8,128)(2,1)} async-done(((bf16[1,64,1152]{2,1,0:T(8,128)(2,1)}), bf16[1,1024,1152]{2,1,0:T(8,128)(2,1)}) %all-gather.52.cloned.1.call-update) | async-done | bytes 2359312 | tf_op jit(solution)/shard_map/all_gather | solution.py:49
  2408.7 44.1 %all-gather.50.cloned.1.call-done = bf16[1,1024,1152]{2,1,0:T(8,128)(2,1)} async-done(((bf16[1,64,1152]{2,1,0:T(8,128)(2,1)}), bf16[1,1024,1152]{2,1,0:T(8,128)(2,1)}) %all-gather.50.cloned.1.call-update) | async-done | bytes 2359312 | tf_op jit(solution)/shard_map/all_gather | solution.py:49
  2452.8 4.3 fusion.595
  2461.0 74.4 %reduce-scatter.65.cloned.1.call-done = bf16[1,64,1152]{2,1,0:T(8,128)(2,1)} async-done(((bf16[1,1024,1152]{2,1,0:T(8,128)(2,1)}), bf16[1,64,1152]{2,1,0:T(8,128)(2,1)}) %reduce-scatter.65.cloned.1.call-update) | async-done | bytes 147472 | tf_op jit(solution)/shard_map/reduce_scatter | solution.py:53
  2543.5 41.2 %all-gather.54.cloned.1.call-done = bf16[1,1024,1152]{2,1,0:T(8,128)(2,1)} async-done(((bf16[1,64,1152]{2,1,0:T(8,128)(2,1)}), bf16[1,1024,1152]{2,1,0:T(8,128)(2,1)}) %all-gather.54.cloned.1.call-update) | async-done | bytes 2359312 | tf_op jit(solution)/shard_map/all_gather | solution.py:49
  2598.7 74.4 %reduce-scatter.67.cloned.1.call-done = bf16[1,64,1152]{2,1,0:T(8,128)(2,1)} async-done(((bf16[1,1024,1152]{2,1,0:T(8,128)(2,1)}), bf16[1,64,1152]{2,1,0:T(8,128)(2,1)}) %reduce-scatter.67.cloned.1.call-update) | async-done | bytes 147472 | tf_op jit(solution)/shard_map/reduce_scatter | solution.py:53
  2677.3 5.7 collective-permute-done.7
  2684.6 4.4 fusion.19
  2689.1 40.4 %all-gather.56.cloned.1.call-done = bf16[1,1024,1152]{2,1,0:T(8,128)(2,1)} async-done(((bf16[1,64,1152]{2,1,0:T(8,128)(2,1)}), bf16[1,1024,1152]{2,1,0:T(8,128)(2,1)}) %all-gather.56.cloned.1.call-update) | async-done | bytes 2359312 | tf_op jit(solution)/shard_map/all_gather | solution.py:49
  2729.5 4.3 fusion.594
  2754.8 52.2 %reduce-scatter.73.cloned.1.call-done = bf16[1,64,1152]{2,1,0:T(8,128)(2,1)} async-done(((bf16[1,1024,1152]{2,1,0:T(8,128)(2,1)}), bf16[1,64,1152]{2,1,0:T(8,128)(2,1)}) %reduce-scatter.73.cloned.1.call-update) | async-done | bytes 147472 | tf_op jit(solution)/shard_map/reduce_scatter | solution.py:53
  2807.0 77.5 %reduce-scatter.69.cloned.1.call-done = bf16[1,64,1152]{2,1,0:T(8,128)(2,1)} async-done(((bf16[1,1024,1152]{2,1,0:T(8,128)(2,1)}), bf16[1,64,1152]{2,1,0:T(8,128)(2,1)}) %reduce-scatter.69.cloned.1.call-update) | async-done | bytes 147472 | tf_op jit(solution)/shard_map/reduce_scatter | solution.py:53
  2925.5 8.5 all-gather.58.cloned.1.call-done
  2944.5 4.9 multiply_convert_fusion
  2969.0 30.8 reduce-scatter.81.cloned.1.call-done
  3004.3 8.0 all-reduce.3
  3012.2 16.8 reduce-scatter.77.cloned.1.call-done
  3030.6 30.0 reduce-scatter.75.cloned.1.call-done
  3062.4 76.4 %reduce-scatter.71.cloned.1.call-done = bf16[1,64,1152]{2,1,0:T(8,128)(2,1)} async-done(((bf16[1,1024,1152]{2,1,0:T(8,128)(2,1)}), bf16[1,64,1152]{2,1,0:T(8,128)(2,1)}) %reduce-scatter.71.cloned.1.call-update) | async-done | bytes 147472 | tf_op jit(solution)/shard_map/reduce_scatter | solution.py:53
  3140.3 326.0 %all-reduce.2 = (f32[2,1152]{1,0:T(2,128)S(1)}, f32[4,1152]{1,0:T(4,128)S(1)}) all-reduce(f32[2,1152]{1,0:T(2,128)S(1)} %fusion.557, f32[4,1152]{1,0:T(4,128)S(1)} %fusion.554), channel_id=27, replica_groups=mesh['section'=2,'fsdp'=4,'tensor'=16] {'fsdp','tensor'}, use_global_device_ids=true, to_apply=%region_101.102.clone | all-reduce | flops 6912 | bytes 55296
  (969 shorter events, 373.0 us)
Async XLA Ops:
  7.2 425.8 %all-gather.22.cloned.1.call-start = ((), (), s32[]{:S(2)}) async-start(), calls=%async_computation.24 | async-start | bytes 2506752 | tf_op jit(solution)/shard_map/all_gather | solution.py:49
  11.0 1674.4 %copy-start.190 = (f32[64]{0:T(128)}, f32[64]{0:T(128)S(1)}, u32[]{:S(2)}) copy-start(f32[64]{0:T(128)S(1)} %broadcast_multiply_fusion.29) | copy-start | bytes 772
  12.1 640.6 %copy-start.235 = (f32[64]{0:T(128)}, f32[64]{0:T(128)S(1)}, u32[]{:S(2)}) copy-start(f32[64]{0:T(128)S(1)} %fusion.358) | copy-start | bytes 772
  390.8 124.1 %reduce-scatter.35.cloned.1.call-start = ((), (), s32[]{:S(2)}) async-start(), calls=%async_computation.25 | async-start | bytes 2506752 | tf_op jit(solution)/shard_map/reduce_scatter | solution.py:53
  413.2 672.4 %copy-start.192 = (f32[72]{0:T(128)}, f32[72]{0:T(128)S(1)}, u32[]{:S(2)}) copy-start(f32[72]{0:T(128)S(1)} %get-tuple-element.147) | copy-start | bytes 868
  413.2 672.4 %copy-start.195 = (f32[72]{0:T(128)}, f32[72]{0:T(128)S(1)}, u32[]{:S(2)}) copy-start(f32[72]{0:T(128)S(1)} %get-tuple-element.148) | copy-start | bytes 868
  435.7 836.9 %copy-start.29 = (bf16[1,1,1024,72]{2,3,0,1:T(8,128)(2,1)}, bf16[1,1,1024,72]{2,3,0,1:T(8,128)(2,1)S(1)}, u32[]{:S(2)}) copy-start(bf16[1,1,1024,72]{2,3,0,1:T(8,128)(2,1)S(1)} %get-tuple-element.128) | copy-start | bytes 442372
  440.5 123.5 %all-gather.24.cloned.1.call-start = ((), (), s32[]{:S(2)}) async-start(), calls=%async_computation.26 | async-start | bytes 2506752 | tf_op jit(solution)/shard_map/all_gather | solution.py:49
  516.1 518.2 %copy-start.228 = (f32[64]{0:T(128)}, f32[64]{0:T(128)S(1)}, u32[]{:S(2)}) copy-start(f32[64]{0:T(128)S(1)} %broadcast_multiply_fusion.28) | copy-start | bytes 772
  517.2 517.0 %copy-start.238 = (f32[64]{0:T(128)}, f32[64]{0:T(128)S(1)}, u32[]{:S(2)}) copy-start(f32[64]{0:T(128)S(1)} %add_rsqrt_fusion.8) | copy-start | bytes 772
  518.9 126.4 %reduce-scatter.37.cloned.1.call-start = ((), (), s32[]{:S(2)}) async-start(), calls=%async_computation.27 | async-start | bytes 2506752 | tf_op jit(solution)/shard_map/reduce_scatter | solution.py:53
  570.9 129.0 %all-gather.26.cloned.1.call-start = ((), (), s32[]{:S(2)}) async-start(), calls=%async_computation.28 | async-start | bytes 2506752 | tf_op jit(solution)/shard_map/all_gather | solution.py:49
  646.3 6.0 collective-permute-start
  652.5 1032.9 %copy-start.186 = (f32[64]{0:T(128)}, f32[64]{0:T(128)S(1)}, u32[]{:S(2)}) copy-start(f32[64]{0:T(128)S(1)} %broadcast_multiply_fusion.27) | copy-start | bytes 772
  653.3 1032.1 %copy-start.188 = (f32[64]{0:T(128)}, f32[64]{0:T(128)S(1)}, u32[]{:S(2)}) copy-start(f32[64]{0:T(128)S(1)} %get-tuple-element.160) | copy-start | bytes 772
  654.1 127.8 %reduce-scatter.39.cloned.1.call-start = ((), (), s32[]{:S(2)}) async-start(), calls=%async_computation.29 | async-start | bytes 2506752 | tf_op jit(solution)/shard_map/reduce_scatter | solution.py:53
  702.5 568.6 %copy-start.7 = (f32[1024,216]{0,1}, f32[1024,216]{0,1:S(1)}, u32[]{:S(2)}) copy-start(f32[1024,216]{0,1:S(1)} %fusion.98) | copy-start | bytes 2654212
  702.7 570.0 %copy-start.25 = (bf16[1,1,1024,72]{2,3,0,1:T(8,128)(2,1)}, bf16[1,1,1024,72]{2,3,0,1:T(8,128)(2,1)S(1)}, u32[]{:S(2)}) copy-start(bf16[1,1,1024,72]{2,3,0,1:T(8,128)(2,1)S(1)} %get-tuple-element.126) | copy-start | bytes 442372
  707.4 124.0 %all-gather.28.cloned.1.call-start = ((), (), s32[]{:S(2)}) async-start(), calls=%async_computation.30 | async-start | bytes 2506752 | tf_op jit(solution)/shard_map/all_gather | solution.py:49
  786.3 92.9 %all-gather.60.cloned.1.call-start = ((), (), s32[]{:S(2)}) async-start(), calls=%async_computation.63 | async-start | bytes 2506752 | tf_op jit(solution)/shard_map/all_gather | solution.py:49
  787.1 169.8 %reduce-scatter.45.cloned.1.call-start = ((), (), s32[]{:S(2)}) async-start(), calls=%async_computation.34 | async-start | bytes 2506752 | tf_op jit(solution)/shard_map/reduce_scatter | solution.py:53
  839.3 194.9 %reduce-scatter.41.cloned.1.call-start = ((), (), s32[]{:S(2)}) async-start(), calls=%async_computation.31 | async-start | bytes 2506752 | tf_op jit(solution)/shard_map/reduce_scatter | solution.py:53
  888.4 194.6 %all-gather.32.cloned.1.call-start = ((), (), s32[]{:S(2)}) async-start(), calls=%async_computation.35 | async-start | bytes 2506752 | tf_op jit(solution)/shard_map/all_gather | solution.py:49
  957.9 76.4 %collective-permute-start.2 = (bf16[1,64,1152]{2,1,0:T(8,128)(2,1)S(1)}, bf16[1,64,1152]{2,1,0:T(8,128)(2,1)S(1)}, u32[]{:S(2)}, u32[]{:S(2)}) collective-permute-start(bf16[1,64,1152]{2,1,0:T(8,128)(2,1)S(1)} %add_convert_fusion.7), channel_id=1, source_target_pairs={{0,64},{1,65},{2,66},{3,67},{4,68},{5,69},{6,70},{7,71},{8,72},{9,... | collective-permute-start | bytes 442376 | tf_op jit(solution)/shard_map/ppermute | solution.py:17
  1037.9 127.2 %reduce-scatter.47.cloned.1.call-start = ((), (), s32[]{:S(2)}) async-start(), calls=%async_computation.36 | async-start | bytes 2506752 | tf_op jit(solution)/shard_map/reduce_scatter | solution.py:53
  1090.6 124.5 %all-gather.36.cloned.1.call-start = ((), (), s32[]{:S(2)}) async-start(), calls=%async_computation.38 | async-start | bytes 2506752 | tf_op jit(solution)/shard_map/all_gather | solution.py:49
  1170.0 92.8 %all-gather.30.cloned.1.call-start = ((), (), s32[]{:S(2)}) async-start(), calls=%async_computation.32 | async-start | bytes 2506752 | tf_op jit(solution)/shard_map/all_gather | solution.py:49
  1170.8 169.6 %reduce-scatter.53.cloned.1.call-start = ((), (), s32[]{:S(2)}) async-start(), calls=%async_computation.42 | async-start | bytes 2506752 | tf_op jit(solution)/shard_map/reduce_scatter | solution.py:53
  1222.0 195.8 %reduce-scatter.43.cloned.1.call-start = ((), (), s32[]{:S(2)}) async-start(), calls=%async_computation.33 | async-start | bytes 2506752 | tf_op jit(solution)/shard_map/reduce_scatter | solution.py:53
  1275.9 190.0 %all-gather.40.cloned.1.call-start = ((), (), s32[]{:S(2)}) async-start(), calls=%async_computation.43 | async-start | bytes 2506752 | tf_op jit(solution)/shard_map/all_gather | solution.py:49
  1341.4 76.4 %collective-permute-start.4 = (bf16[1,64,1152]{2,1,0:T(8,128)(2,1)S(1)}, bf16[1,64,1152]{2,1,0:T(8,128)(2,1)S(1)}, u32[]{:S(2)}, u32[]{:S(2)}) collective-permute-start(bf16[1,64,1152]{2,1,0:T(8,128)(2,1)S(1)} %add_convert_fusion.5), channel_id=1, source_target_pairs={{0,64},{1,65},{2,66},{3,67},{4,68},{5,69},{6,70},{7,71},{8,72},{9,... | collective-permute-start | bytes 442376 | tf_op jit(solution)/shard_map/ppermute | solution.py:17
  1420.7 127.1 %reduce-scatter.55.cloned.1.call-start = ((), (), s32[]{:S(2)}) async-start(), calls=%async_computation.44 | async-start | bytes 2506752 | tf_op jit(solution)/shard_map/reduce_scatter | solution.py:53
  1473.4 123.6 %all-gather.44.cloned.1.call-start = ((), (), s32[]{:S(2)}) async-start(), calls=%async_computation.46 | async-start | bytes 2506752 | tf_op jit(solution)/shard_map/all_gather | solution.py:49
  1551.8 126.5 %reduce-scatter.61.cloned.1.call-start = ((), (), s32[]{:S(2)}) async-start(), calls=%async_computation.50 | async-start | bytes 2506752 | tf_op jit(solution)/shard_map/reduce_scatter | solution.py:53
  1603.9 132.3 %all-gather.48.cloned.1.call-start = ((), (), s32[]{:S(2)}) async-start(), calls=%async_computation.51 | async-start | bytes 2506752 | tf_op jit(solution)/shard_map/all_gather | solution.py:49
  1679.3 6.0 collective-permute-start.6
  1690.3 93.7 %all-gather.34.cloned.1.call-start = ((), (), s32[]{:S(2)}) async-start(), calls=%async_computation.37 | async-start | bytes 2506752 | tf_op jit(solution)/shard_map/all_gather | solution.py:49
  1690.4 7.2 collective-permute-start.1
  1699.0 162.7 %reduce-scatter.63.cloned.1.call-start = ((), (), s32[]{:S(2)}) async-start(), calls=%async_computation.52 | async-start | bytes 2506752 | tf_op jit(solution)/shard_map/reduce_scatter | solution.py:53
  1744.4 194.7 %reduce-scatter.49.cloned.1.call-start = ((), (), s32[]{:S(2)}) async-start(), calls=%async_computation.39 | async-start | bytes 2506752 | tf_op jit(solution)/shard_map/reduce_scatter | solution.py:53
  1792.1 197.2 %all-gather.38.cloned.1.call-start = ((), (), s32[]{:S(2)}) async-start(), calls=%async_computation.40 | async-start | bytes 2506752 | tf_op jit(solution)/shard_map/all_gather | solution.py:49
  1944.3 134.7 %reduce-scatter.51.cloned.1.call-start = ((), (), s32[]{:S(2)}) async-start(), calls=%async_computation.41 | async-start | bytes 2506752 | tf_op jit(solution)/shard_map/reduce_scatter | solution.py:53
  2004.5 130.6 %all-gather.42.cloned.1.call-start = ((), (), s32[]{:S(2)}) async-start(), calls=%async_computation.45 | async-start | bytes 2506752 | tf_op jit(solution)/shard_map/all_gather | solution.py:49
  2082.2 7.0 collective-permute-start.3
  2090.0 127.7 %reduce-scatter.57.cloned.1.call-start = ((), (), s32[]{:S(2)}) async-start(), calls=%async_computation.47 | async-start | bytes 2506752 | tf_op jit(solution)/shard_map/reduce_scatter | solution.py:53
  2143.2 124.5 %all-gather.46.cloned.1.call-start = ((), (), s32[]{:S(2)}) async-start(), calls=%async_computation.48 | async-start | bytes 2506752 | tf_op jit(solution)/shard_map/all_gather | solution.py:49
  2222.6 134.6 %reduce-scatter.59.cloned.1.call-start = ((), (), s32[]{:S(2)}) async-start(), calls=%async_computation.49 | async-start | bytes 2506752 | tf_op jit(solution)/shard_map/reduce_scatter | solution.py:53
  2282.7 122.2 %all-gather.52.cloned.1.call-start = ((), (), s32[]{:S(2)}) async-start(), calls=%async_computation.54 | async-start | bytes 2506752 | tf_op jit(solution)/shard_map/all_gather | solution.py:49
  2283.5 169.3 %all-gather.50.cloned.1.call-start = ((), (), s32[]{:S(2)}) async-start(), calls=%async_computation.53 | async-start | bytes 2506752 | tf_op jit(solution)/shard_map/all_gather | solution.py:49
  2360.3 7.0 collective-permute-start.5
  2368.7 166.7 %reduce-scatter.65.cloned.1.call-start = ((), (), s32[]{:S(2)}) async-start(), calls=%async_computation.55 | async-start | bytes 2506752 | tf_op jit(solution)/shard_map/reduce_scatter | solution.py:53
  2460.9 123.8 %all-gather.54.cloned.1.call-start = ((), (), s32[]{:S(2)}) async-start(), calls=%async_computation.56 | async-start | bytes 2506752 | tf_op jit(solution)/shard_map/all_gather | solution.py:49
  2539.6 133.5 %reduce-scatter.67.cloned.1.call-start = ((), (), s32[]{:S(2)}) async-start(), calls=%async_computation.57 | async-start | bytes 2506752 | tf_op jit(solution)/shard_map/reduce_scatter | solution.py:53
  2598.6 130.9 %all-gather.56.cloned.1.call-start = ((), (), s32[]{:S(2)}) async-start(), calls=%async_computation.58 | async-start | bytes 2506752 | tf_op jit(solution)/shard_map/all_gather | solution.py:49
  2676.0 7.0 collective-permute-start.7
  2684.4 122.6 %reduce-scatter.73.cloned.1.call-start = ((), (), s32[]{:S(2)}) async-start(), calls=%async_computation.62 | async-start | bytes 2506752 | tf_op jit(solution)/shard_map/reduce_scatter | solution.py:53
  2689.1 195.4 %reduce-scatter.69.cloned.1.call-start = ((), (), s32[]{:S(2)}) async-start(), calls=%async_computation.59 | async-start | bytes 2506752 | tf_op jit(solution)/shard_map/reduce_scatter | solution.py:53
  2738.1 195.9 %all-gather.58.cloned.1.call-start = ((), (), s32[]{:S(2)}) async-start(), calls=%async_computation.60 | async-start | bytes 2506752 | tf_op jit(solution)/shard_map/all_gather | solution.py:49
  2888.9 77.8 %reduce-scatter.79.cloned.1.call-start = ((), (), s32[]{:S(2)}) async-start(), calls=%async_computation.66 | async-start | bytes 1105920
  2914.1 85.6 %reduce-scatter.81.cloned.1.call-start = ((), (), s32[]{:S(2)}) async-start(), calls=%async_computation.67 | async-start | bytes 1105920
  2925.4 103.6 %reduce-scatter.77.cloned.1.call-start = ((), (), s32[]{:S(2)}) async-start(), calls=%async_computation.65 | async-start | bytes 368640
  2951.8 108.8 %reduce-scatter.75.cloned.1.call-start = ((), (), s32[]{:S(2)}) async-start(), calls=%async_computation.64 | async-start | bytes 737280
  2956.1 182.7 %reduce-scatter.71.cloned.1.call-start = ((), (), s32[]{:S(2)}) async-start(), calls=%async_computation.61 | async-start | bytes 2506752 | tf_op jit(solution)/shard_map/reduce_scatter | solution.py:53
  3004.0 464.8 %copy-start.132 = (bf16[1,64,1152]{2,1,0:T(8,128)(2,1)S(1)}, bf16[1,64,1152]{2,1,0:T(8,128)(2,1)}, u32[]{:S(2)}) copy-start(bf16[1,64,1152]{2,1,0:T(8,128)(2,1)} %copy-done.131) | copy-start | bytes 442372
  (273 other events, 11239.8 us)
Sparse Core Ops, SparseCore 0:
  391.0 42.0 all-gather.21
  440.6 74.2 reduce-scatter.34
  519.1 44.9 all-gather.23
  571.0 74.2 reduce-scatter.36
  654.2 45.6 all-gather.25
  707.5 74.3 reduce-scatter.38
  786.5 44.9 all-gather.27
  834.2 45.0 all-gather.59
  882.6 74.2 reduce-scatter.44
  960.0 74.1 reduce-scatter.40
  1038.0 44.9 all-gather.31
  1090.7 74.3 reduce-scatter.46
  1170.1 44.9 all-gather.35
  1217.7 45.0 all-gather.29
  1266.0 74.4 reduce-scatter.52
  1343.6 74.1 reduce-scatter.42
  1420.8 44.9 all-gather.39
  1473.5 74.3 reduce-scatter.54
  1551.9 44.9 all-gather.43
  1604.0 74.2 reduce-scatter.60
  1690.5 45.6 all-gather.47
  1738.9 45.0 all-gather.33
  1787.3 74.2 reduce-scatter.62
  1864.8 74.1 reduce-scatter.48
  1944.4 44.9 all-gather.37
  2004.6 74.2 reduce-scatter.50
  2090.1 44.9 all-gather.41
  2143.3 74.2 reduce-scatter.56
  2222.7 44.9 all-gather.45
  2282.8 74.2 reduce-scatter.58
  2360.0 44.8 all-gather.51
  2407.7 45.0 all-gather.49
  2461.0 74.2 reduce-scatter.64
  2539.7 44.9 all-gather.53
  2598.7 74.2 reduce-scatter.66
  2684.5 44.9 all-gather.55
  2732.7 74.2 reduce-scatter.72
  2810.3 74.1 reduce-scatter.68
  2889.0 44.9 all-gather.57
  2936.7 29.9 reduce-scatter.78
  2969.5 30.1 reduce-scatter.80
  3002.3 26.6 reduce-scatter.76
  3032.2 28.3 reduce-scatter.74
  3064.3 74.5 reduce-scatter.70
where the time goes:
time: 3480 us
  waiting for transfers between devices  2300 us (66%)
  blocking collectives  721 us (21%)
  matrix products  220 us (6%)
  local copies, waits for them, and re-layouts  102 us (3%)
  other arithmetic  95.9 us (3%)
    reduce_scatter x20, waiting for transfers between devices, collect_rows(): lax.psum_scatter(summand.astype(jnp.bfloat16), 'tensor', scatter_dimensio...  1440 us
    all_gather x20, waiting for transfers between devices, spread_rows(): return lax.all_gather(rows_low, 'tensor', axis=1, tiled=True)  741 us
    unnamed x1, blocking collectives  326 us
    all_gather x1, blocking collectives, body(): lax.all_gather(shifts, ('fsdp', 'tensor'), axis=2, tiled=True)  172 us
    all_gather x1, blocking collectives, body(): lax.all_gather(gains, ('fsdp', 'tensor'), axis=2, tiled=True)  163 us
    unnamed x48, waiting for transfers between devices  81 us
  transfers between devices with their start and end apart: 52, of which 50 were waited for; matrix products, arithmetic and copies ran while one was open for 5% of the time, Pallas kernels for 0%

commit v1 on v0

v1 whole, which is shorter than its diff:
```python
import functools

import jax
import jax.numpy as jnp
from jax import lax
from jax.experimental import pallas as pl
from jax.experimental.pallas import tpu as pltpu
from jax.sharding import Mesh
from jax.sharding import PartitionSpec as P

AXES = ("xl", "xh", "c", "y", "z")
EPSILON = 1e-06
BF = jnp.bfloat16
F32 = jnp.float32
LANES = 128
CHEAP = pl.CostEstimate(flops=1 << 20, bytes_accessed=1 << 16, transcendentals=0)


def swap(value, axis):
    return lax.ppermute(value, axis, [(0, 1), (1, 0)])


def pick(flag, if_true, if_false):
    return jnp.where(flag, if_true, if_false)


def dot(spec, left, right):
    return jnp.einsum(spec, left, right, preferred_element_type=F32)


def norm_rows(hidden, gain_row, offset_row):
    average = jnp.mean(hidden, axis=-1, keepdims=True)
    centered = hidden - average
    inv_spread = lax.rsqrt(jnp.mean(centered * centered, axis=-1, keepdims=True) + EPSILON)
    normed = centered * inv_spread
    return (normed * gain_row + offset_row).astype(BF), normed, inv_spread


def norm_back(carried, grad_normed, normed, inv_spread, gain_row):
    scaled = grad_normed * gain_row
    inner_mean = jnp.mean(scaled, axis=-1, keepdims=True)
    cross_mean = jnp.mean(scaled * normed, axis=-1, keepdims=True)
    grad_hidden = carried + inv_spread * (scaled - inner_mean - normed * cross_mean)
    return grad_hidden, jnp.sum(grad_normed * normed, axis=0), jnp.sum(grad_normed, axis=0)


def gelu_tanh(values):
    return jax.nn.gelu(values, approximate=True)


def product(left, right, left_dim, right_dim):
    return lax.dot_general(left, right, (((left_dim,), (right_dim,)), ((), ())), preferred_element_type=F32)


def probabilities(query, keys, scale):
    scores = [product(key, query, 1, 1) * scale for key in keys]
    top = jnp.maximum(*(jnp.max(block, axis=0, keepdims=True) for block in scores))
    raised = [jnp.exp(block - top) for block in scores]
    weight = 1.0 / sum(jnp.sum(block, axis=0, keepdims=True) for block in raised)
    return [block * weight for block in raised]


def head(ref, index):
    return ref[:, index * LANES : (index + 1) * LANES]


def attend_kernel(scale, query, own, other, out):
    for h in range(4):
        probs = probabilities(head(query, h), (head(own, h), head(other, h)), scale)
        mixed = product(head(own, 4 + h), probs[0].astype(BF), 0, 0)
        mixed += product(head(other, 4 + h), probs[1].astype(BF), 0, 0)
        out[:, h * LANES : (h + 1) * LANES] = mixed.T.astype(BF)


def attend_back_kernel(scale, query, own, other, grad, grad_query, sum_query, grad_own, grad_other):
    for h in range(4):
        place = slice(h * LANES, (h + 1) * LANES)
        rows, pull = head(query, h), head(grad, h)
        keys = head(own, h), head(other, h)
        probs = probabilities(rows, keys, scale)
        pulled = [product(head(ref, 4 + h), pull, 1, 1) for ref in (own, other)]
        mean = sum(jnp.sum(p * g, axis=0, keepdims=True) for p, g in zip(probs, pulled))
        scores = [(p * (g - mean)).astype(BF) for p, g in zip(probs, pulled)]
        turned = sum(product(key, block, 0, 0) for key, block in zip(keys, scores))
        from_query = turned.T * scale
        grad_query[:, place] = from_query.astype(BF)
        sum_query[:, place] = jnp.sum(from_query, axis=0, keepdims=True)
        for result, p, s in zip((grad_own, grad_other), probs, scores):
            result[0, :, place] = (product(s, rows, 1, 0) * scale).astype(result.dtype)
            result[1, :, place] = product(p.astype(BF), pull, 1, 0).astype(result.dtype)


def on_vmem(kernel, out_shape, limit, *args, flags=0):
    vmem = pl.BlockSpec(memory_space=pltpu.VMEM)
    return pl.pallas_call(
        kernel,
        in_specs=[pl.BlockSpec(memory_space=pltpu.SMEM)] * flags + [vmem] * (len(args) - flags),
        out_specs=jax.tree.map(lambda _: vmem, out_shape),
        out_shape=out_shape,
        compiler_params=pltpu.CompilerParams(vmem_limit_bytes=limit << 20),
        cost_estimate=CHEAP,
    )(*args)


def attend(query, own, other, hd):
    out = jax.ShapeDtypeStruct(query.shape, BF)
    return on_vmem(functools.partial(attend_kernel, hd**-0.5), out, 24, query, own, other)


def attend_back(query, own, other, grad, hd):
    rows, width = query.shape
    out = [
        jax.ShapeDtypeStruct((rows, width), BF),
        jax.ShapeDtypeStruct((1, width), F32),
        jax.ShapeDtypeStruct((2, rows, width), F32),
        jax.ShapeDtypeStruct((2, rows, width), BF),
    ]
    return on_vmem(functools.partial(attend_back_kernel, hd**-0.5), out, 24, query, own, other, grad)


def outer_kernel(with_sum, tile, flag, left_one, right_one, left_two, right_two, *rest):
    out = rest[-1]

    def result(left, right):
        def step(index, carry):
            place = pl.ds(pl.multiple_of(index * tile, LANES), tile)
            total = product(left[...], right[:, place], 0, 0)
            if with_sum:
                total += rest[0][:, place].astype(F32)
            out[:, place] = total.astype(out.dtype)
            return carry

        lax.fori_loop(0, out.shape[1] // tile, step, 0)

    @pl.when(flag[0] == 1)
    def _():
        result(left_one, right_one)

    @pl.when(flag[0] != 1)
    def _():
        result(left_two, right_two)


def outer(flag, one, two, summand=None):
    units, width = one[0].shape[1], one[1].shape[1]
    tile = width // 3 if width % 384 == 0 else width
    extra = [] if summand is None else [summand]
    kernel = functools.partial(outer_kernel, bool(extra), tile)
    out = jax.ShapeDtypeStruct((units, width), BF)
    return on_vmem(kernel, out, 24, flag, *one, *two, *extra, flags=1)


def cut_kernel(first, second, out):
    quarter = out.shape[2]
    for layer, part in enumerate((first, second)):
        for i in range(4):
            out[layer * 4 + i] = part[:, i * quarter : (i + 1) * quarter].astype(BF)


def owned_mask(piece, devices, width):
    column = lax.broadcasted_iota(jnp.int32, (devices, width), 1)
    start = lax.broadcasted_iota(jnp.int32, (devices, width), 0) * piece
    return jnp.logical_and(column >= start, column < start + piece)


def exact(left, chosen):
    high = left.astype(BF)
    rest = left - high.astype(F32)
    middle = rest.astype(BF)
    low = (rest - middle.astype(F32)).astype(BF)
    return sum(product(part, chosen, 1, 0) for part in (low, middle, high))


def unpack_kernel(piece, phase, table, out):
    devices, width = table.shape[0] // 2, phase.shape[1]
    mask = owned_mask(piece, devices, width)
    lane = lax.broadcasted_iota(jnp.int32, (LANES, width), 0)
    for vector in range(out.shape[0]):
        spread = exact(table[...], (lane - vector * piece == phase[...]).astype(BF))
        for layer in range(2):
            rows = spread[layer * devices : (layer + 1) * devices]
            out[vector, layer : layer + 1] = jnp.sum(jnp.where(mask, rows, 0.0), axis=0, keepdims=True)


def pack_kernel(piece, phase, grads, out):
    devices, width = out.shape[1], phase.shape[0]
    mask = owned_mask(piece, devices, width)
    lane = lax.broadcasted_iota(jnp.int32, (width, LANES), 1)
    for layer in range(2):
        total = jnp.zeros((devices, LANES), F32)
        for vector in range(grads.shape[0]):
            rows = jnp.broadcast_to(grads[vector, layer : layer + 1], (devices, width))
            total += exact(jnp.where(mask, rows, 0.0), (lane - vector * piece == phase[...]).astype(BF))
        out[layer] = total


def unpack_vectors(table, width):
    piece = width // 64
    phase = (jnp.arange(width, dtype=jnp.int32) % piece)[None]
    out = jax.ShapeDtypeStruct((6, 2, width), F32)
    return on_vmem(functools.partial(unpack_kernel, piece), out, 16, phase, table)


def pack_vectors(grads):
    width = grads.shape[2]
    piece = width // 64
    phase = (jnp.arange(width, dtype=jnp.int32) % piece)[:, None]
    out = jax.ShapeDtypeStruct((2, 64, LANES), F32)
    return on_vmem(functools.partial(pack_kernel, piece), out, 16, phase, grads)


def tie(*values):
    return lax.optimization_barrier(values)


def ring(value, axis, step):
    return lax.ppermute(value, axis, [(i, (i + step) % 4) for i in range(4)])


def spread_near(rows):
    return ring(rows, "z", 1), ring(rows, "z", -1)


def spread_far(near):
    below, above = near
    half = below.shape[0] // 2
    return ring(below[:half], "z", 1), ring(above[half:], "z", -1)


def join(rows, near, far):
    return jnp.concatenate([rows, *near, *far], axis=0)


def chunks_of(summand):
    count = summand.shape[0] // 4
    low = summand.astype(BF)
    return [low[i * count : (i + 1) * count] for i in range(4)]


def collect_far(chunks, axis="z"):
    far = chunks[3]
    half = far.shape[0] // 2
    return ring(far[:half], axis, 1), ring(far[half:], axis, -1)


def collect_near(chunks, passed, axis="z"):
    own, below, above, _ = chunks
    half = own.shape[0] // 2
    above_one = (above[:half].astype(F32) + passed[0].astype(F32)).astype(BF)
    below_two = (below[half:].astype(F32) + passed[1].astype(F32)).astype(BF)
    from_below = ring(jnp.concatenate([above_one, above[half:]], axis=0), axis, 1)
    from_above = ring(jnp.concatenate([below[:half], below_two], axis=0), axis, -1)
    return own.astype(F32) + from_below.astype(F32) + from_above.astype(F32)


def pad_heads(rows, hd):
    return jnp.pad(rows, ((0, 0), (0, LANES - hd), (0, 0))).reshape(4 * LANES, rows.shape[2])


def attn_weights(own, other, on_first):
    first, second = pick(on_first, own, other), pick(on_first, other, own)
    hd = own.shape[1] // 2
    w_query = pad_heads(first[:, :hd], hd)
    w_pair = jnp.concatenate([pad_heads(first[:, hd:], hd), pad_heads(second[:, :hd], hd)])
    return w_query, w_pair, pad_heads(second[:, hd:], hd)


def mlp_weights(own, other, on_first):
    shape = (-1, own.shape[2])
    return pick(on_first, own, other).reshape(shape), pick(on_first, other, own).reshape(shape)


def from_owners(part):
    rows, quarter = part.shape[1:]
    sent = jnp.broadcast_to(part[None], (4, 2, rows, quarter)).reshape(8, rows, quarter)
    arrived = lax.all_to_all(sent, ("xl", "xh", "c"), 0, 0).reshape(2, 4, rows, quarter)
    return [jnp.concatenate([arrived[layer, i] for i in range(4)], axis=-1) for layer in range(2)]


def to_owners(parts):
    rows, width = parts[0].shape
    out = jax.ShapeDtypeStruct((8, rows, width // 4), BF)
    chunks = on_vmem(cut_kernel, out, 16, *parts)
    arrived = lax.all_to_all(chunks, ("xl", "xh", "c"), 0, 0)
    return jnp.sum(arrived.reshape(4, 2, rows, width // 4).astype(F32), axis=0)


def by_xor(values, index):
    odd, high = index % 2 == 1, index >= 2
    values = [pick(odd, values[i ^ 1], values[i]) for i in range(4)]
    return [pick(high, values[i ^ 2], values[i]) for i in range(4)]


def token_routes():
    routes = []
    for step in range(4):
        route = []
        for a in range(2):
            for b in range(2):
                for y in range(4):
                    m = (2 * a + y % 2) ^ step
                    route.append(((a * 2 + b) * 4 + y, (b * 2 + y // 2) * 4 + m))
        routes.append(route)
    return routes


def x_ring():
    order = [xl_at * 2 + xh_at for xh_at in range(2) for xl_at in range(2)]
    up = [(order[i], order[(i + 1) % 4]) for i in range(4)]
    return up, [(b, a) for a, b in up]


def from_owners_ring(part, on_first):
    kept, given = pick(on_first, part[0], part[1]), pick(on_first, part[1], part[0])
    got = swap(given, "c")
    block = jnp.concatenate([pick(on_first, kept, got), pick(on_first, got, kept)], axis=-1)
    half = block.shape[0] // 2
    up, down = x_ring()
    below, above = lax.ppermute(block, ("xl", "xh"), up), lax.ppermute(block, ("xl", "xh"), down)
    far = jnp.concatenate(
        [lax.ppermute(below[:half], ("xl", "xh"), up), lax.ppermute(above[half:], ("xl", "xh"), down)]
    )
    turn = 2 * lax.axis_index("xh") + lax.axis_index("xl")

    def source(x):
        away = (x - turn) % 4
        return pick(away == 0, block, pick(away == 1, above, pick(away == 2, far, below)))

    return [jnp.concatenate([source(layer), source(layer + 2)], axis=-1) for layer in range(2)]


def forward_layer(hidden, rows1, attn_own, mlp_own, vectors, b_query, b_pair, b_up, hd, on_first, attn_other, late, beside):
    w_query, w_pair, w_out = attn_weights(attn_own, attn_other, on_first)
    own = (dot("nd,fd->nf", rows1, w_pair) + b_pair).astype(BF)
    other = swap(own, "c")
    query = (dot("nd,fd->nf", rows1, w_query) + b_query).astype(BF)
    attn = attend(query, own, other, hd)
    attn, beside = tie(attn, beside)
    chunks = chunks_of(dot("nf,fd->nd", attn, w_out))
    passed, mlp_own = tie(collect_far(chunks), mlp_own)
    branch, mlp_other = tie(collect_near(chunks, passed), swap(mlp_own, "c"))
    middle = hidden + (branch + vectors[3])
    a2, unit2, rstd2 = norm_rows(middle, vectors[1], vectors[4])
    near, (w_up, w_down) = tie(spread_near(a2), mlp_weights(mlp_own, mlp_other, on_first))
    rows2 = join(a2, near, spread_far(near))
    pre = dot("nd,kd->nk", rows2, w_up) + b_up
    act = gelu_tanh(pre).astype(BF)
    stored = (rows1, query, own, other, attn, unit2, rstd2, rows2, pre, act)
    weights = (w_query, w_pair, w_out, w_up, w_down)
    if late is None:
        return middle, stored, weights, beside
    chunks = chunks_of(dot("nk,kd->nd", act, w_down))
    summed, held = tie(collect_near(chunks, collect_far(chunks)), late(mlp_own))
    result = middle + (summed + vectors[5])
    return result, stored, weights, held, beside


def backward_layer(grad_out, down_rows, stored, unit_rows, unit1, rstd1, weights, vectors, on_first, hd, beside, to_owner):
    rows1, query, own, other, attn, unit2, rstd2, rows2, pre, act = stored
    w_query, w_pair, w_out, w_up, w_down = weights
    grad_act = dot("nd,kd->nk", down_rows, w_down)
    grad_pre = jax.vjp(gelu_tanh, pre)[1](grad_act)[0]
    pre_low = grad_pre.astype(BF)
    summand = dot("nk,kd->nd", pre_low, w_up).astype(BF)
    if beside is not None:
        beside = chunks_of(dot("nk,kd->nd", beside, w_down))
        summand, pre_low, beside_passed = tie(summand, pre_low, collect_far(beside))
    else:
        summand, pre_low = tie(summand, pre_low)
    chunks = chunks_of(summand)
    up_pair, down_pair = (pre_low, rows2), (act, down_rows)
    flag = on_first.astype(jnp.int32).reshape(1)
    ga2, given = tie(collect_near(chunks, collect_far(chunks)), outer(flag, down_pair, up_pair))
    grad_middle, gain2, offset2 = norm_back(grad_out, ga2, unit2, rstd2, vectors[1])
    go = grad_middle.astype(BF)
    near, part_mlp = tie(spread_near(go), outer(flag, up_pair, down_pair, swap(given, "c")))
    part_mlp = lax.psum_scatter(part_mlp.reshape(4, -1, part_mlp.shape[1]), "y", scatter_dimension=0, tiled=False)
    far = spread_far(near)
    if beside is not None:
        far, beside_passed = tie(far, beside_passed)
    out_rows = join(go, near, far)
    gattn = dot("nd,fd->nf", out_rows, w_out).astype(BF)
    grad_query, sum_query, grad_own, grad_other = attend_back(query, own, other, gattn, hd)
    if beside is not None:
        grad_other, beside = tie(grad_other, collect_near(beside, beside_passed))
    sent = swap(grad_other, "c")
    grad_w_out = dot("nf,nd->fd", attn, out_rows).astype(BF)
    grad_w_query = dot("nf,nd->fd", grad_query, rows1).astype(BF)
    from_query = dot("nf,fd->nd", grad_query, w_query)
    sent, part_mlp, grad_w_out, grad_w_query, from_query = tie(sent, part_mlp, grad_w_out, grad_w_query, from_query)
    pair = grad_own + sent.astype(F32)
    sum_value = jnp.sum(pair[1], axis=0)
    pair = pair.astype(BF)
    partial = from_query + dot("nf,fd->nd", jnp.concatenate([pair[0], pair[1]], axis=1), w_pair)
    gain1, offset1 = jnp.sum(partial * unit_rows, axis=0), jnp.sum(partial, axis=0)
    chunks = chunks_of(partial)

    def heads(rows):
        return rows.reshape(4, LANES, -1)[:, :hd]

    def attn_grads(pair):
        grad_w_key, grad_w_value = (dot("nf,nd->fd", pair[i], rows1).astype(BF) for i in range(2))
        first = jnp.concatenate([heads(grad_w_query), heads(grad_w_key)], axis=1)
        second = jnp.concatenate([heads(grad_w_value), heads(grad_w_out)], axis=1)
        return pick(on_first, second, first), pick(on_first, first, second)

    passed, pair, part_mlp = tie(collect_far(chunks), pair, part_mlp)
    given, kept = attn_grads(pair)
    part_mlp = to_owner(part_mlp)
    part_attn = (kept.astype(F32) + swap(given, "c").astype(F32)).astype(BF)
    ga1, gain1, offset1 = tie(collect_near(chunks, passed), gain1, offset1)
    grad_hidden = norm_back(grad_middle, ga1, unit1, rstd1, vectors[0])[0]
    grad_vectors = [gain1, gain2, offset1, jnp.sum(grad_middle, axis=0), offset2, jnp.sum(grad_out, axis=0)]
    grad_b_up = jnp.sum(grad_pre, axis=0)
    grad_b_qv = jnp.stack([sum_query[0], sum_value]).reshape(2, 4, LANES)
    return grad_hidden, part_attn, part_mlp, (grad_vectors, grad_b_qv, grad_b_up), beside


def body(ends_in, w_qkv, b_qv, w_out, w_up, b_up, w_down, gains, shifts):
    xl, core, own_y, own_z = (lax.axis_index(axis) for axis in ("xl", "c", "y", "z"))
    local = ends_in[0, :, 0]
    _, rows, width = local.shape
    hd = w_qkv.shape[3]
    units = w_up.shape[2]
    padded = -(-units // 16) * 16
    spare = padded - units

    on_first = core == 0
    qkv_rows = jnp.transpose(w_qkv[0], (1, 2, 0))
    pad_rows = ((0, spare), (0, 0))
    attn_rows = jnp.stack([qkv_rows[:2].reshape(2 * hd, -1), jnp.concatenate([qkv_rows[2], w_out[0]], axis=0)])
    mlp_rows = jnp.stack([jnp.pad(w_up[0].T, pad_rows), jnp.pad(w_down[0], pad_rows)])
    attn_rows, local = tie(attn_rows, local)
    attn_parts = from_owners(attn_rows)

    place = 2 * xl + own_y % 2
    routes = token_routes()
    blocks = by_xor([local[m] for m in range(4)], place)
    blocks = [lax.ppermute(block, ("xl", "c", "y"), route) for block, route in zip(blocks, routes)]
    blocks = by_xor(blocks, own_y)
    start_low, cot_low = jnp.concatenate(blocks[:2]), jnp.concatenate(blocks[2:])
    piece = width // 64
    up_lines = -(-padded // LANES)
    lines = -(-(3 + up_lines) // 8) * 8

    def line(values, count):
        return jnp.pad(values, (0, count * LANES - values.shape[0])).reshape(count, LANES)

    own = [line(jnp.concatenate([gains[0].ravel(), shifts[0].ravel()]), 1), line(b_qv[0, 0], 1), line(b_qv[0, 1], 1)]
    own = jnp.concatenate(own + [line(b_up[0], lines - 3)])[None]
    near = spread_near(start_low)
    own, attn0_part, mlp_rows = tie(own, attn_parts[0], mlp_rows)
    attn0_own = lax.all_gather(attn0_part, "y", axis=0)
    table = lax.all_to_all(jnp.broadcast_to(own, (128, lines, LANES)), AXES, 0, 0)
    start_rows = join(start_low, near, spread_far(near))
    mlp_parts = from_owners_ring(mlp_rows, on_first)
    attn0_own, mlp_parts, attn1_part = tie(attn0_own, mlp_parts, attn_parts[1])
    mlp0_own = lax.all_gather(mlp_parts[0], "y", axis=0)
    part1 = jnp.concatenate([attn1_part, mlp_parts[1]])

    vectors = jnp.swapaxes(unpack_vectors(table[:, 0], width), 0, 1)
    biases = lax.dynamic_index_in_dim(table.reshape(2, 4, 4, 4, lines, LANES)[:, 0], own_z, 2, keepdims=False)
    bias_qv = biases[:, :, 1:3].transpose(0, 2, 1, 3)
    bias_up = biases[:, :, 3 : 3 + up_lines].reshape(2, 4, -1)[..., :padded].reshape(2, -1)
    bias_qv = bias_qv.reshape(2, 2, 4 * LANES)
    bias_pair = jnp.concatenate([jnp.zeros_like(bias_qv[:, 1]), bias_qv[:, 1]], axis=-1)

    start, cotangent = start_low.astype(F32), cot_low.astype(F32)
    rows0, unit_rows0, _ = norm_rows(start_rows.astype(F32), vectors[0, 0], vectors[0, 2])
    _, unit0, rstd0 = norm_rows(start, vectors[0, 0], vectors[0, 2])
    def fetch_next(after):
        own = tie(after, part1)[1]
        return lax.all_gather(own, "y", axis=0)

    middle, stored0, weights0, own1, cot_near = forward_layer(
        start, rows0, attn0_own, mlp0_own, vectors[0], bias_qv[0, 0], bias_pair[0], bias_up[0], hd, on_first,
        swap(attn0_own, "c"), fetch_next, spread_near(cot_low),
    )
    attn1_own, mlp1_own = own1[:, : 2 * hd], own1[:, 2 * hd :]
    middle = middle.astype(BF)
    near, attn1_own, attn1_other = tie(spread_near(middle), attn1_own, swap(attn1_own, "c"))
    middle_rows = join(middle, near, spread_far(near)).astype(F32)
    middle = middle.astype(F32)
    rows1, unit_rows1, _ = norm_rows(middle_rows, vectors[1, 0], vectors[1, 2])
    _, unit1, rstd1 = norm_rows(middle, vectors[1, 0], vectors[1, 2])
    middle1, stored1, weights1, cot_far = forward_layer(
        middle, rows1, attn1_own, mlp1_own, vectors[1], bias_qv[1, 0], bias_pair[1], bias_up[1], hd, on_first,
        attn1_other, None, spread_far(cot_near),
    )
    down_rows = join(cot_low, cot_near, cot_far)
    grad1, attn1, mlp1, small1, branch = backward_layer(
        cotangent, down_rows, stored1, unit_rows1, unit1, rstd1, weights1, vectors[1], on_first, hd,
        stored1[-1], lambda part: part,
    )
    result = middle1 + (branch + vectors[1, 5])
    grad1 = grad1.astype(BF)
    near, attn1 = tie(spread_near(grad1), attn1)
    attn1 = lax.psum_scatter(attn1, "y", scatter_dimension=0, tiled=False)
    down_rows = join(grad1, near, spread_far(near))
    grad0, attn0, grad_mlp, small0, _ = backward_layer(
        grad1.astype(F32), down_rows, stored0, unit_rows0, unit0, rstd0, weights0, vectors[0], on_first, hd, None,
        lambda part: to_owners((part, mlp1)),
    )
    gvec1, gqv1, gup1 = small1
    gvec0, gqv0, gup0 = small0

    chunks = [lax.dynamic_index_in_dim(attn0, (own_y + step) % 4, 0, keepdims=False) for step in (0, 3, 1, 2)]
    half = rows
    out_grad, out_result = grad0.astype(BF), result.astype(BF)
    blocks = by_xor([out_grad[:half], out_grad[half:], out_result[:half], out_result[half:]], own_y)
    passed, blocks = tie(collect_far(chunks, "y"), blocks)
    attn0 = collect_near(chunks, passed, "y")
    blocks = [
        lax.ppermute(block, ("xl", "c", "y"), [(b, a) for a, b in route]) for block, route in zip(blocks, routes)
    ]
    ends_out = jnp.stack(by_xor(blocks, place))

    grad_vectors = jnp.stack(gvec0 + gvec1).reshape(2, 6, width).swapaxes(0, 1)
    grad_qv = jnp.stack([gqv0, gqv1]).transpose(0, 2, 1, 3)
    grad_up = jnp.stack([gup0, gup1]).reshape(2, 4, padded)
    grad_up = jnp.pad(grad_up, ((0, 0), (0, 0), (0, (lines - 3) * LANES - padded)))
    grad_bias = jnp.concatenate([grad_qv, grad_up.reshape(2, 4, lines - 3, LANES)], axis=2)
    here = (jnp.arange(4) == own_z)[:, None, None]
    grad_bias = jnp.where(here, grad_bias[:, None, :, None], 0.0)
    grad_bias = jnp.broadcast_to(grad_bias, (2, 4, 4, 4, lines - 1, LANES)).reshape(128, lines - 1, LANES)
    sent = jnp.concatenate([pack_vectors(grad_vectors).reshape(128, 1, LANES), grad_bias], axis=1)
    owned = lax.all_to_all(sent, AXES, 0, 0)

    grad_attn = to_owners((attn0, attn1))
    owned = jnp.sum(owned, axis=0)
    share_vec = owned[0, : 6 * piece].reshape(6, piece)
    share_qv = owned[1:3, :hd]
    share_b_up = owned[3:].reshape(-1)[:units]
    share_up = grad_mlp[0, :units].T
    share_down = grad_mlp[1, :units]
    heads = grad_attn.reshape(4, hd, -1)
    share_qkv = jnp.transpose(heads[:3], (2, 0, 1))
    share_out = heads[3]

    return (
        ends_out[None, :, None],
        share_qkv[None],
        share_qv[None],
        share_out[None],
        share_up[None],
        share_b_up[None],
        share_down[None],
        share_vec[None, :2],
        share_vec[None, 2:],
    )


def solution(mesh):
    fine = Mesh(mesh.devices.reshape(2, 2, 2, 4, 4), AXES)
    f, t = ("xh", "c"), ("y", "z")
    specs = (
        P("xl", None, f, t, None),
        P("xl", f, None, t),
        P("xl", None, t),
        P("xl", t, f),
        P("xl", f, t),
        P("xl", t),
        P("xl", t, f),
        P("xl", None, f + t),
        P("xl", None, f + t),
    )
    return jax.shard_map(body, mesh=fine, in_specs=specs, out_specs=specs, check_vma=False)
```

time: 3480 us -> 562 us (0.16)
  waiting for transfers between devices: 2300 us -> 149 us
  blocking collectives: 721 us -> 0 us
  matrix products: 220 us -> 52.1 us
  starting transfers between devices: 23.4 us -> 168 us
  Pallas kernels: 0 us -> 46 us
  local copies, waits for them, and re-layouts: 102 us -> 62.1 us
  other arithmetic: 95.9 us -> 56.5 us
    reduce_scatter x20 -> x3, waiting for transfers between devices: 1440 us -> 3.64 us  [the longest x2 3.62 us: backward_layer(): lax.psum_scatter(part_mlp.reshape(4, -1, part_mlp.shape[1]), 'y', scatter...]
    all_gather x20 -> x3, waiting for transfers between devices: 741 us -> 9.29 us  [the longest x1 9.28 us: body(): mlp0_own = lax.all_gather(mlp_parts[0], 'y', axis=0)]
    all_gather x6 -> x0, blocking collectives: 387 us -> none  [the longest x1 172 us: body(): lax.all_gather(shifts, ('fsdp', 'tensor'), axis=2, tiled=True)]
    unnamed x1 -> x0, blocking collectives: 326 us -> none
    dot_general x85 -> x28, matrix products: 197 us -> 52.1 us  [dot(): return jnp.einsum(spec, left, right, preferred_element_type=F32)]
    ppermute x8 -> x93, starting transfers between devices: 18.7 us -> 132 us  [the longest x68 116 us: ring(): return lax.ppermute(value, axis, [(i, (i + step) % 4) for i in range(4)])]
    unnamed x48 -> x6, waiting for transfers between devices: 81 us -> 0.1 us
    ppermute x8 -> x93, waiting for transfers between devices: 27.8 us -> 106 us  [the longest x68 102 us: ring(): return lax.ppermute(value, axis, [(i, (i + step) % 4) for i in range(4)])]
  transfers between devices with their start and end apart: 52 -> 104, of which waited for: 50 -> 47; matrix products, arithmetic and copies ran while one was open for 5% -> 21% of each run, Pallas kernels for 0% -> 8%
where the time goes in v1:
time: 562 us; the launch traced here: 552 us
  starting transfers between devices  168 us (30%)
  waiting for transfers between devices  149 us (27%)
  local copies, waits for them, and re-layouts  62.1 us (11%)
  other arithmetic  56.5 us (10%)
  matrix products  52.1 us (9%)
  Pallas kernels  46 us (8%)
  between operations  17.9 us (3%)
    ppermute x68, starting transfers between devices, ring(): return lax.ppermute(value, axis, [(i, (i + step) % 4) for i in range(4)])  116 us
    ppermute x68, waiting for transfers between devices, ring(): return lax.ppermute(value, axis, [(i, (i + step) % 4) for i in range(4)])  102 us
    dot_general x28, matrix products, dot(): return jnp.einsum(spec, left, right, preferred_element_type=F32)  52.1 us
    pallas_call x12, Pallas kernels, on_vmem(): pl.pallas_call(kernel, in_specs=[pl.BlockSpec(memory_space=pltpu.SMEM)] *...  46 us
    unnamed x392, local copies, waits for them, and re-layouts  28.3 us
    all_to_all x2, waiting for transfers between devices, to_owners(): arrived = lax.all_to_all(chunks, ('xl', 'xh', 'c'), 0, 0)  19.3 us
    all_to_all x2, starting transfers between devices, to_owners(): arrived = lax.all_to_all(chunks, ('xl', 'xh', 'c'), 0, 0)  11.9 us
  transfers between devices with their start and end apart: 104, of which 47 were waited for; matrix products, arithmetic and copies ran while one was open for 21% of the time, Pallas kernels for 8%

profile of v1, /device:TPU:0, one launch (start us, length us, event | category | flops | bytes accessed | tf_op | source)
XLA Modules:
  0.0 551.8 jit_solution(11019161595627636035)
XLA Ops:
  10.0 3.2 collective-permute-start
  16.1 8.1 %all-to-all-start = ((bf16[8,144,288]{2,1,0:T(8,128)(2,1)}), bf16[8,144,288]{2,1,0:T(8,128)(2,1)}, u32[]{:S(2)}, u32[]{:S(2)}) async-start(bf16[8,144,288]{2,1,0:T(8,128)(2,1)} %bitcast.19), calls=%async_computation | async-start | bytes 1769472 | tf_op jit(solution)/shard_map/all_to_all | solution.py:276
  30.6 7.5 %collective-permute-done.4 = bf16[128,1152]{1,0:T(8,128)(2,1)S(1)} collective-permute-done((bf16[128,1152]{1,0:T(8,128)(2,1)S(1)}, bf16[128,1152]{1,0:T(8,128)(2,1)S(1)}, u32[]{:S(2)}, u32[]{:S(2)}) %collective-permute-start.4) | collective-permute-done | bytes 294944 | tf_op jit(solution)/shard_map/ppermute | solution.py:217
  39.6 3.2 collective-permute-start.7
  55.5 8.1 %all-to-all-start.1 = ((f32[128,8,128]{2,1,0:T(8,128)}), f32[128,8,128]{2,1,0:T(8,128)}, u32[]{:S(2)}, u32[]{:S(2)}) async-start(f32[128,8,128]{2,1,0:T(8,128)} %broadcast_in_dim.47), calls=%async_computation.1 | async-start | bytes 1048576 | tf_op jit(solution)/shard_map/all_to_all | solution.py:454
  68.5 2.4 collective-permute-start.12
  71.9 3.0 collective-permute-done.11
  96.6 4.2 shard_map.161
  107.3 3.3 collective-permute-done.17
  110.6 9.3 %all-gather.9.cloned.1.call-done = bf16[1088,1152]{1,0:T(8,128)(2,1)} async-done(((bf16[272,1152]{1,0:T(8,128)(2,1)}), bf16[1088,1152]{1,0:T(8,128)(2,1)}) %all-gather.9.cloned.1.call-update) | async-done | bytes 2506768 | tf_op jit(solution)/shard_map/all_gather | solution.py:458
  127.4 5.0 collective-permute-done.19
  140.9 4.4 collective-permute-done.22
  146.4 2.3 collective-permute-start.25
  148.7 3.0 collective-permute-done.24
  151.7 3.5 multiply_convert_fusion.1
  160.6 3.0 collective-permute-done.26
  167.3 4.6 collective-permute-done.27
  179.2 7.3 %collective-permute-done.30 = bf16[128,1152]{1,0:T(8,128)(2,1)S(1)} collective-permute-done((bf16[128,1152]{1,0:T(8,128)(2,1)S(1)}, bf16[128,1152]{1,0:T(8,128)(2,1)S(1)}, u32[]{:S(2)}, u32[]{:S(2)}) %collective-permute-start.30) | collective-permute-done | bytes 294944 | tf_op jit(solution)/shard_map/ppermute | solution.py:217
  197.3 2.2 collective-permute-start.37
  200.7 4.2 shard_map.162
  206.9 3.1 collective-permute-start.39
  215.7 3.0 collective-permute-start.41
  218.8 7.2 %collective-permute-done.40 = bf16[128,1152]{1,0:T(8,128)(2,1)S(1)} collective-permute-done((bf16[128,1152]{1,0:T(8,128)(2,1)S(1)}, bf16[128,1152]{1,0:T(8,128)(2,1)S(1)}, u32[]{:S(2)}, u32[]{:S(2)}) %collective-permute-start.40) | collective-permute-done | bytes 294944 | tf_op jit(solution)/shard_map/ppermute | solution.py:217
  232.7 6.1 %collective-permute-done.43 = bf16[128,1152]{1,0:T(8,128)(2,1)S(1)} collective-permute-done((bf16[128,1152]{1,0:T(8,128)(2,1)S(1)}, bf16[128,1152]{1,0:T(8,128)(2,1)S(1)}, u32[]{:S(2)}, u32[]{:S(2)}) %collective-permute-start.43) | collective-permute-done | bytes 294944 | tf_op jit(solution)/shard_map/ppermute | solution.py:217
  240.2 2.5 collective-permute-start.46
  245.9 3.8 fusion.95
  262.4 3.1 collective-permute-done.49
  273.4 2.3 shard_map.163
  283.3 4.0 shard_map.164
  287.4 3.3 collective-permute-done.53
  293.7 2.8 collective-permute-start.57
  296.6 3.3 collective-permute-done.56
  301.8 2.7 collective-permute-start.59
  307.3 8.3 %shard_map.165 = (bf16[512,512]{1,0:T(8,128)(2,1)S(1)}, f32[1,512]{1,0:T(1,128)S(1)}, f32[2,512,512]{2,1,0:T(8,128)S(1)}, bf16[2,512,512]{2,1,0:T(8,128)(2,1)S(1)}) custom-call(bf16[512,512]{1,0:T(8,128)(2,1)S(1)} %copy-done.17, bf16[512,1024]{1,0:T(8,128)(2,1)S(1)} %copy-done.11, bf16[512,1024]{1,0:T(8,128)(2,1)S(1)} %copy-done.13, ...), custom_call_target="tpu_custom_call" | custom-call | flops 1048576 | bytes 65536 | tf_op jit(solution)/shard_map/pallas_call | solution.py:95
  322.0 2.3 fusion.113
  324.6 3.1 fusion.98
  335.1 3.7 collective-permute-done.61
  344.9 4.5 collective-permute-done.63
  351.7 2.3 collective-permute-start.66
  356.7 2.9 collective-permute-done.65
  363.5 2.7 collective-permute-start.69
  369.2 4.5 fusion.93
  379.2 3.9 collective-permute-done.70
  387.3 2.3 shard_map.166
  389.7 2.2 collective-permute-done.71
  398.4 3.9 shard_map.167
  402.3 3.5 collective-permute-done.74
  409.1 2.4 collective-permute-start.78
  416.0 2.3 convolution_convert_fusion.14.grad
  418.3 9.3 %shard_map.168 = (bf16[512,512]{1,0:T(8,128)(2,1)S(1)}, f32[1,512]{1,0:T(1,128)S(1)}, f32[2,512,512]{2,1,0:T(8,128)S(1)}, bf16[2,512,512]{2,1,0:T(8,128)(2,1)}) custom-call(bf16[512,512]{1,0:T(8,128)(2,1)S(1)} %copy-done.15, bf16[512,1024]{1,0:T(8,128)(2,1)S(1)} %copy-done.7, bf16[512,1024]{1,0:T(8,128)(2,1)S(1)} %copy-done.9, ...), custom_call_target="tpu_custom_call" | custom-call | flops 1048576 | bytes 65536 | tf_op jit(solution)/shard_map/pallas_call | solution.py:95
  428.2 3.4 convolution_convert_fusion.3
  433.7 2.3 fusion.114
  436.0 3.2 reduce-scatter.6.cloned.1.call-done
  448.6 3.3 collective-permute-done.80
  461.8 2.8 shard_map.170
  465.7 8.0 %all-to-all-start.3 = ((f32[128,8,128]{2,1,0:T(8,128)}), f32[128,8,128]{2,1,0:T(8,128)S(1)}, u32[]{:S(2)}, u32[]{:S(2)}) async-start(f32[128,8,128]{2,1,0:T(8,128)} %pad_maximum_fusion.17), calls=%async_computation.6 | async-start | bytes 1048576 | tf_op jit(solution)/shard_map/all_to_all | solution.py:527
  475.6 10.6 %all-to-all-done.3 = f32[128,8,128]{2,1,0:T(8,128)S(1)} async-done(((f32[128,8,128]{2,1,0:T(8,128)}), f32[128,8,128]{2,1,0:T(8,128)S(1)}, u32[]{:S(2)}, u32[]{:S(2)}) %all-to-all-start.3) | async-done | bytes 524320 | tf_op jit(solution)/shard_map/all_to_all | solution.py:527
  486.2 3.6 all-to-all-start.4
  495.0 2.6 collective-permute-start.84
  498.1 4.1 collective-permute-done.83
  502.6 3.2 collective-permute-start.92
  505.8 6.4 %all-to-all-done.4 = bf16[8,272,288]{2,1,0:T(8,128)(2,1)S(1)} async-done(((bf16[8,272,288]{2,1,0:T(8,128)(2,1)}), bf16[8,272,288]{2,1,0:T(8,128)(2,1)S(1)}, u32[]{:S(2)}, u32[]{:S(2)}) %all-to-all-start.4) | async-done | bytes 1253408 | tf_op jit(solution)/shard_map/all_to_all | solution.py:284
  520.7 8.3 %all-to-all-start.2 = ((bf16[8,144,288]{2,1,0:T(8,128)(2,1)}), bf16[8,144,288]{2,1,0:T(8,128)(2,1)S(1)}, u32[]{:S(2)}, u32[]{:S(2)}) async-start(bf16[8,144,288]{2,1,0:T(8,128)(2,1)} %shard_map.169), calls=%async_computation.5 | async-start | bytes 1769472 | tf_op jit(solution)/shard_map/all_to_all | solution.py:284
  530.1 12.9 %all-to-all-done.2 = bf16[8,144,288]{2,1,0:T(8,128)(2,1)S(1)} async-done(((bf16[8,144,288]{2,1,0:T(8,128)(2,1)}), bf16[8,144,288]{2,1,0:T(8,128)(2,1)S(1)}, u32[]{:S(2)}, u32[]{:S(2)}) %all-to-all-start.2) | async-done | bytes 663584 | tf_op jit(solution)/shard_map/all_to_all | solution.py:284
  (822 shorter events, 256.0 us)
Async XLA Ops:
  10.0 14.7 %collective-permute-start = (bf16[64,1152]{1,0:T(8,128)(2,1)S(1)}, bf16[64,1152]{1,0:T(8,128)(2,1)S(1)}, u32[]{:S(2)}, u32[]{:S(2)}) collective-permute-start(bf16[64,1152]{1,0:T(8,128)(2,1)S(1)} %get-tuple-element.415), channel_id=1, source_target_pairs={{0,12},{4,8},{8,28},{12,24},{16,76},{20,72},{24,92},{28,88},{64,4}... | collective-permute-start | bytes 442376 | tf_op jit(solution)/shard_map/ppermute | solution.py:439
  13.2 11.6 %collective-permute-start.1 = (bf16[64,1152]{1,0:T(8,128)(2,1)S(1)}, bf16[64,1152]{1,0:T(8,128)(2,1)S(1)}, u32[]{:S(2)}, u32[]{:S(2)}) collective-permute-start(bf16[64,1152]{1,0:T(8,128)(2,1)S(1)} %get-tuple-element.412), channel_id=1, source_target_pairs={{0,8},{4,12},{8,24},{12,28},{16,72},{20,76},{24,88},{28,92},{64,0}... | collective-permute-start | bytes 442376 | tf_op jit(solution)/shard_map/ppermute | solution.py:439
  14.1 10.7 %collective-permute-start.2 = (bf16[64,1152]{1,0:T(8,128)(2,1)S(1)}, bf16[64,1152]{1,0:T(8,128)(2,1)S(1)}, u32[]{:S(2)}, u32[]{:S(2)}) collective-permute-start(bf16[64,1152]{1,0:T(8,128)(2,1)S(1)} %get-tuple-element.413), channel_id=1, source_target_pairs={{0,4},{4,0},{8,20},{12,16},{16,68},{20,64},{24,84},{28,80},{64,12}... | collective-permute-start | bytes 442376 | tf_op jit(solution)/shard_map/ppermute | solution.py:439
  14.3 10.5 %collective-permute-start.3 = (bf16[64,1152]{1,0:T(8,128)(2,1)S(1)}, bf16[64,1152]{1,0:T(8,128)(2,1)S(1)}, u32[]{:S(2)}, u32[]{:S(2)}) collective-permute-start(bf16[64,1152]{1,0:T(8,128)(2,1)S(1)} %get-tuple-element.414), channel_id=1, source_target_pairs={{0,0},{4,4},{8,16},{12,20},{16,64},{20,68},{24,80},{28,84},{64,8},... | collective-permute-start | bytes 442376 | tf_op jit(solution)/shard_map/ppermute | solution.py:439
  16.1 26.7 %all-to-all-start = ((bf16[8,144,288]{2,1,0:T(8,128)(2,1)}), bf16[8,144,288]{2,1,0:T(8,128)(2,1)}, u32[]{:S(2)}, u32[]{:S(2)}) async-start(bf16[8,144,288]{2,1,0:T(8,128)(2,1)} %bitcast.19), calls=%async_computation | async-start | bytes 1769472 | tf_op jit(solution)/shard_map/all_to_all | solution.py:276
  24.2 54.4 %all-gather.7.cloned.1.call-start = ((), (), s32[]{:S(2)}) async-start(), calls=%async_computation.11 | async-start | bytes 1658880 | tf_op jit(solution)/shard_map/all_gather | solution.py:453
  26.4 11.7 %collective-permute-start.4 = (bf16[128,1152]{1,0:T(8,128)(2,1)S(1)}, bf16[128,1152]{1,0:T(8,128)(2,1)S(1)}, u32[]{:S(2)}, u32[]{:S(2)}) collective-permute-start(bf16[128,1152]{1,0:T(8,128)(2,1)S(1)} %pad_maximum_fusion.22), channel_id=1, source_target_pairs={{0,1},{1,2},{2,3},{3,0},{4,5},{5,6},{6,7},{7,4},{8,9},{9,10},{10,1... | collective-permute-start | bytes 884744 | tf_op jit(solution)/shard_map/ppermute | solution.py:217
  28.4 10.5 %collective-permute-start.5 = (bf16[128,1152]{1,0:T(8,128)(2,1)S(1)}, bf16[128,1152]{1,0:T(8,128)(2,1)S(1)}, u32[]{:S(2)}, u32[]{:S(2)}) collective-permute-start(bf16[128,1152]{1,0:T(8,128)(2,1)S(1)} %pad_maximum_fusion.22), channel_id=1, source_target_pairs={{0,3},{1,0},{2,1},{3,2},{4,7},{5,4},{6,5},{7,6},{8,11},{9,8},{10,9... | collective-permute-start | bytes 884744 | tf_op jit(solution)/shard_map/ppermute | solution.py:217
  38.8 26.8 %collective-permute-start.6 = (bf16[64,1152]{1,0:T(8,128)(2,1)}, bf16[64,1152]{1,0:T(8,128)(2,1)}, u32[]{:S(2)}, u32[]{:S(2)}) collective-permute-start(bf16[64,1152]{1,0:T(8,128)(2,1)} %slice.782), channel_id=1, source_target_pairs={{0,1},{1,2},{2,3},{3,0},{4,5},{5,6},{6,7},{7,4},{8,9},{9,10},{10,1... | collective-permute-start | bytes 442376 | tf_op jit(solution)/shard_map/ppermute | solution.py:217
  39.6 31.4 %collective-permute-start.7 = (bf16[64,1152]{1,0:T(8,128)(2,1)}, bf16[64,1152]{1,0:T(8,128)(2,1)}, u32[]{:S(2)}, u32[]{:S(2)}) collective-permute-start(bf16[64,1152]{1,0:T(8,128)(2,1)} %slice.783), channel_id=1, source_target_pairs={{0,3},{1,0},{2,1},{3,2},{4,7},{5,4},{6,5},{7,6},{8,11},{9,8},{10,9... | collective-permute-start | bytes 442376 | tf_op jit(solution)/shard_map/ppermute | solution.py:217
  50.4 16.2 %collective-permute-start.10 = (bf16[272,576]{1,0:T(8,128)(2,1)}, bf16[272,576]{1,0:T(8,128)(2,1)S(1)}, u32[]{:S(2)}, u32[]{:S(2)}) collective-permute-start(bf16[272,576]{1,0:T(8,128)(2,1)} %pad_maximum_fusion.19), channel_id=1, source_target_pairs={{0,64},{64,32},{32,96},{96,0},{1,65},{65,33},{33,97},{97,1},{2,66}... | collective-permute-start | bytes 940040 | tf_op jit(solution)/shard_map/ppermute | solution.py:319
  52.1 15.5 %collective-permute-start.9 = (bf16[272,576]{1,0:T(8,128)(2,1)}, bf16[272,576]{1,0:T(8,128)(2,1)}, u32[]{:S(2)}, u32[]{:S(2)}) collective-permute-start(bf16[272,576]{1,0:T(8,128)(2,1)} %pad_maximum_fusion.19), channel_id=1, source_target_pairs={{64,0},{32,64},{96,32},{0,96},{65,1},{33,65},{97,33},{1,97},{66,2}... | collective-permute-start | bytes 940040 | tf_op jit(solution)/shard_map/ppermute | solution.py:319
  55.5 23.8 %all-to-all-start.1 = ((f32[128,8,128]{2,1,0:T(8,128)}), f32[128,8,128]{2,1,0:T(8,128)}, u32[]{:S(2)}, u32[]{:S(2)}) async-start(f32[128,8,128]{2,1,0:T(8,128)} %broadcast_in_dim.47), calls=%async_computation.1 | async-start | bytes 1048576 | tf_op jit(solution)/shard_map/all_to_all | solution.py:454
  63.5 56.3 %all-gather.9.cloned.1.call-start = ((), (), s32[]{:S(2)}) async-start(), calls=%async_computation.12 | async-start | bytes 3133440 | tf_op jit(solution)/shard_map/all_gather | solution.py:458
  66.6 8.2 %collective-permute-start.11 = (bf16[136,576]{1,0:T(8,128)(2,1)S(1)}, bf16[136,576]{1,0:T(8,128)(2,1)S(1)}, u32[]{:S(2)}, u32[]{:S(2)}) collective-permute-start(bf16[136,576]{1,0:T(8,128)(2,1)S(1)} %slice.791), channel_id=1, source_target_pairs={{0,64},{64,32},{32,96},{96,0},{1,65},{65,33},{33,97},{97,1},{2,66}... | collective-permute-start | bytes 470024 | tf_op jit(solution)/shard_map/ppermute | solution.py:321
  83.8 89.7 %all-gather.11.cloned.1.call-start = ((), (), s32[]{:S(2)}) async-start(), calls=%async_computation.13 | async-start | bytes 4792320 | tf_op jit(solution)/shard_map/all_gather | solution.py:473
  91.2 10.7 %collective-permute-start.15 = (bf16[128,1152]{1,0:T(8,128)(2,1)S(1)}, bf16[128,1152]{1,0:T(8,128)(2,1)S(1)}, u32[]{:S(2)}, u32[]{:S(2)}) collective-permute-start(bf16[128,1152]{1,0:T(8,128)(2,1)S(1)} %pad_maximum_fusion.23), channel_id=1, source_target_pairs={{0,1},{1,2},{2,3},{3,0},{4,5},{5,6},{6,7},{7,4},{8,9},{9,10},{10,1... | collective-permute-start | bytes 884744 | tf_op jit(solution)/shard_map/ppermute | solution.py:217
  92.9 9.0 %collective-permute-start.16 = (bf16[128,1152]{1,0:T(8,128)(2,1)S(1)}, bf16[128,1152]{1,0:T(8,128)(2,1)S(1)}, u32[]{:S(2)}, u32[]{:S(2)}) collective-permute-start(bf16[128,1152]{1,0:T(8,128)(2,1)S(1)} %pad_maximum_fusion.23), channel_id=1, source_target_pairs={{0,3},{1,0},{2,1},{3,2},{4,7},{5,4},{6,5},{7,6},{8,11},{9,8},{10,9... | collective-permute-start | bytes 884744 | tf_op jit(solution)/shard_map/ppermute | solution.py:217
  119.9 13.8 %collective-permute-start.21 = (bf16[4,272,1152]{2,1,0:T(8,128)(2,1)}, bf16[4,272,1152]{2,1,0:T(8,128)(2,1)}, u32[]{:S(2)}, u32[]{:S(2)}) collective-permute-start(bf16[4,272,1152]{2,1,0:T(8,128)(2,1)} %bitcast.258), channel_id=1, source_target_pairs={{0,16},{16,0},{1,17},{17,1},{2,18},{18,2},{3,19},{19,3},{4,20},{20... | collective-permute-start | bytes 7520264 | tf_op jit(solution)/shard_map/ppermute | solution.py:20
  121.6 10.8 %collective-permute-start.19 = (bf16[128,1152]{1,0:T(8,128)(2,1)S(1)}, bf16[128,1152]{1,0:T(8,128)(2,1)}, u32[]{:S(2)}, u32[]{:S(2)}) collective-permute-start(bf16[128,1152]{1,0:T(8,128)(2,1)S(1)} %pad_maximum_fusion.24), channel_id=1, source_target_pairs={{0,1},{1,2},{2,3},{3,0},{4,5},{5,6},{6,7},{7,4},{8,9},{9,10},{10,1... | collective-permute-start | bytes 884744 | tf_op jit(solution)/shard_map/ppermute | solution.py:217
  123.2 9.2 %collective-permute-start.20 = (bf16[128,1152]{1,0:T(8,128)(2,1)S(1)}, bf16[128,1152]{1,0:T(8,128)(2,1)S(1)}, u32[]{:S(2)}, u32[]{:S(2)}) collective-permute-start(bf16[128,1152]{1,0:T(8,128)(2,1)S(1)} %pad_maximum_fusion.25), channel_id=1, source_target_pairs={{0,3},{1,0},{2,1},{3,2},{4,7},{5,4},{6,5},{7,6},{8,11},{9,8},{10,9... | collective-permute-start | bytes 884744 | tf_op jit(solution)/shard_map/ppermute | solution.py:217
  127.3 197.3 %reduce-scatter.4.cloned.1.call-start = ((), (), s32[]{:S(2)}) async-start(), calls=%async_computation.8 | async-start | bytes 3133440 | tf_op jit(solution)/shard_map/reduce_scatter | solution.py:377
  135.3 9.9 %collective-permute-start.22 = (bf16[128,1152]{1,0:T(8,128)(2,1)S(1)}, bf16[128,1152]{1,0:T(8,128)(2,1)S(1)}, u32[]{:S(2)}, u32[]{:S(2)}) collective-permute-start(bf16[128,1152]{1,0:T(8,128)(2,1)S(1)} %get-tuple-element.308), channel_id=1, source_target_pairs={{0,1},{1,2},{2,3},{3,0},{4,5},{5,6},{6,7},{7,4},{8,9},{9,10},{10,1... | collective-permute-start | bytes 884744 | tf_op jit(solution)/shard_map/ppermute | solution.py:217
  137.0 8.2 %collective-permute-start.23 = (bf16[128,1152]{1,0:T(8,128)(2,1)S(1)}, bf16[128,1152]{1,0:T(8,128)(2,1)S(1)}, u32[]{:S(2)}, u32[]{:S(2)}) collective-permute-start(bf16[128,1152]{1,0:T(8,128)(2,1)S(1)} %get-tuple-element.308), channel_id=1, source_target_pairs={{0,3},{1,0},{2,1},{3,2},{4,7},{5,4},{6,5},{7,6},{8,11},{9,8},{10,9... | collective-permute-start | bytes 884744 | tf_op jit(solution)/shard_map/ppermute | solution.py:217
  163.9 8.0 %collective-permute-start.27 = (bf16[128,1152]{1,0:T(8,128)(2,1)S(1)}, bf16[128,1152]{1,0:T(8,128)(2,1)S(1)}, u32[]{:S(2)}, u32[]{:S(2)}) collective-permute-start(bf16[128,1152]{1,0:T(8,128)(2,1)S(1)} %pad_maximum_fusion.26), channel_id=1, source_target_pairs={{0,1},{1,2},{2,3},{3,0},{4,5},{5,6},{6,7},{7,4},{8,9},{9,10},{10,1... | collective-permute-start | bytes 884744 | tf_op jit(solution)/shard_map/ppermute | solution.py:217
  175.1 11.4 %collective-permute-start.32 = (bf16[4,144,1152]{2,1,0:T(8,128)(2,1)S(1)}, bf16[4,144,1152]{2,1,0:T(8,128)(2,1)S(1)}, u32[]{:S(2)}, u32[]{:S(2)}) collective-permute-start(bf16[4,144,1152]{2,1,0:T(8,128)(2,1)S(1)} %slice.670), channel_id=1, source_target_pairs={{0,16},{16,0},{1,17},{17,1},{2,18},{18,2},{3,19},{19,3},{4,20},{20... | collective-permute-start | bytes 3981320 | tf_op jit(solution)/shard_map/ppermute | solution.py:20
  175.9 10.6 %collective-permute-start.30 = (bf16[128,1152]{1,0:T(8,128)(2,1)S(1)}, bf16[128,1152]{1,0:T(8,128)(2,1)S(1)}, u32[]{:S(2)}, u32[]{:S(2)}) collective-permute-start(bf16[128,1152]{1,0:T(8,128)(2,1)S(1)} %get-tuple-element.294), channel_id=1, source_target_pairs={{0,1},{1,2},{2,3},{3,0},{4,5},{5,6},{6,7},{7,4},{8,9},{9,10},{10,1... | collective-permute-start | bytes 884744 | tf_op jit(solution)/shard_map/ppermute | solution.py:217
  177.4 9.1 %collective-permute-start.31 = (bf16[128,1152]{1,0:T(8,128)(2,1)S(1)}, bf16[128,1152]{1,0:T(8,128)(2,1)S(1)}, u32[]{:S(2)}, u32[]{:S(2)}) collective-permute-start(bf16[128,1152]{1,0:T(8,128)(2,1)S(1)} %get-tuple-element.294), channel_id=1, source_target_pairs={{0,3},{1,0},{2,1},{3,2},{4,7},{5,4},{6,5},{7,6},{8,11},{9,8},{10,9... | collective-permute-start | bytes 884744 | tf_op jit(solution)/shard_map/ppermute | solution.py:217
  195.9 9.0 %collective-permute-start.36 = (bf16[64,1152]{1,0:T(8,128)(2,1)S(1)}, bf16[64,1152]{1,0:T(8,128)(2,1)S(1)}, u32[]{:S(2)}, u32[]{:S(2)}) collective-permute-start(bf16[64,1152]{1,0:T(8,128)(2,1)S(1)} %slice.680), channel_id=1, source_target_pairs={{0,1},{1,2},{2,3},{3,0},{4,5},{5,6},{6,7},{7,4},{8,9},{9,10},{10,1... | collective-permute-start | bytes 442376 | tf_op jit(solution)/shard_map/ppermute | solution.py:217
  197.3 7.6 %collective-permute-start.37 = (bf16[64,1152]{1,0:T(8,128)(2,1)S(1)}, bf16[64,1152]{1,0:T(8,128)(2,1)S(1)}, u32[]{:S(2)}, u32[]{:S(2)}) collective-permute-start(bf16[64,1152]{1,0:T(8,128)(2,1)S(1)} %slice.681), channel_id=1, source_target_pairs={{0,3},{1,0},{2,1},{3,2},{4,7},{5,4},{6,5},{7,6},{8,11},{9,8},{10,9... | collective-permute-start | bytes 442376 | tf_op jit(solution)/shard_map/ppermute | solution.py:217
  214.0 13.1 %collective-permute-start.42 = (bf16[4,272,1152]{2,1,0:T(8,128)(2,1)S(1)}, bf16[4,272,1152]{2,1,0:T(8,128)(2,1)S(1)}, u32[]{:S(2)}, u32[]{:S(2)}) collective-permute-start(bf16[4,272,1152]{2,1,0:T(8,128)(2,1)S(1)} %slice.687), channel_id=1, source_target_pairs={{0,16},{16,0},{1,17},{17,1},{2,18},{18,2},{3,19},{19,3},{4,20},{20... | collective-permute-start | bytes 7520264 | tf_op jit(solution)/shard_map/ppermute | solution.py:20
  215.4 10.7 %collective-permute-start.40 = (bf16[128,1152]{1,0:T(8,128)(2,1)S(1)}, bf16[128,1152]{1,0:T(8,128)(2,1)S(1)}, u32[]{:S(2)}, u32[]{:S(2)}) collective-permute-start(bf16[128,1152]{1,0:T(8,128)(2,1)S(1)} %pad_maximum_fusion.28), channel_id=1, source_target_pairs={{0,1},{1,2},{2,3},{3,0},{4,5},{5,6},{6,7},{7,4},{8,9},{9,10},{10,1... | collective-permute-start | bytes 884744 | tf_op jit(solution)/shard_map/ppermute | solution.py:217
  215.7 10.3 %collective-permute-start.41 = (bf16[128,1152]{1,0:T(8,128)(2,1)S(1)}, bf16[128,1152]{1,0:T(8,128)(2,1)S(1)}, u32[]{:S(2)}, u32[]{:S(2)}) collective-permute-start(bf16[128,1152]{1,0:T(8,128)(2,1)S(1)} %pad_maximum_fusion.29), channel_id=1, source_target_pairs={{0,3},{1,0},{2,1},{3,2},{4,7},{5,4},{6,5},{7,6},{8,11},{9,8},{10,9... | collective-permute-start | bytes 884744 | tf_op jit(solution)/shard_map/ppermute | solution.py:217
  229.0 9.9 %collective-permute-start.43 = (bf16[128,1152]{1,0:T(8,128)(2,1)S(1)}, bf16[128,1152]{1,0:T(8,128)(2,1)S(1)}, u32[]{:S(2)}, u32[]{:S(2)}) collective-permute-start(bf16[128,1152]{1,0:T(8,128)(2,1)S(1)} %get-tuple-element.304), channel_id=1, source_target_pairs={{0,1},{1,2},{2,3},{3,0},{4,5},{5,6},{6,7},{7,4},{8,9},{9,10},{10,1... | collective-permute-start | bytes 884744 | tf_op jit(solution)/shard_map/ppermute | solution.py:217
  230.3 8.6 %collective-permute-start.44 = (bf16[128,1152]{1,0:T(8,128)(2,1)S(1)}, bf16[128,1152]{1,0:T(8,128)(2,1)S(1)}, u32[]{:S(2)}, u32[]{:S(2)}) collective-permute-start(bf16[128,1152]{1,0:T(8,128)(2,1)S(1)} %get-tuple-element.304), channel_id=1, source_target_pairs={{0,3},{1,0},{2,1},{3,2},{4,7},{5,4},{6,5},{7,6},{8,11},{9,8},{10,9... | collective-permute-start | bytes 884744 | tf_op jit(solution)/shard_map/ppermute | solution.py:217
  266.8 9.0 %collective-permute-start.50 = (bf16[128,1152]{1,0:T(8,128)(2,1)}, bf16[128,1152]{1,0:T(8,128)(2,1)}, u32[]{:S(2)}, u32[]{:S(2)}) collective-permute-start(bf16[128,1152]{1,0:T(8,128)(2,1)} %pad_maximum_fusion.30), channel_id=1, source_target_pairs={{0,1},{1,2},{2,3},{3,0},{4,5},{5,6},{6,7},{7,4},{8,9},{9,10},{10,1... | collective-permute-start | bytes 884744 | tf_op jit(solution)/shard_map/ppermute | solution.py:217
  280.1 10.6 %collective-permute-start.53 = (bf16[128,1152]{1,0:T(8,128)(2,1)S(1)}, bf16[128,1152]{1,0:T(8,128)(2,1)S(1)}, u32[]{:S(2)}, u32[]{:S(2)}) collective-permute-start(bf16[128,1152]{1,0:T(8,128)(2,1)S(1)} %get-tuple-element.298), channel_id=1, source_target_pairs={{0,1},{1,2},{2,3},{3,0},{4,5},{5,6},{6,7},{7,4},{8,9},{9,10},{10,1... | collective-permute-start | bytes 884744 | tf_op jit(solution)/shard_map/ppermute | solution.py:217
  281.3 10.2 %collective-permute-start.54 = (bf16[128,1152]{1,0:T(8,128)(2,1)S(1)}, bf16[128,1152]{1,0:T(8,128)(2,1)S(1)}, u32[]{:S(2)}, u32[]{:S(2)}) collective-permute-start(bf16[128,1152]{1,0:T(8,128)(2,1)S(1)} %get-tuple-element.298), channel_id=1, source_target_pairs={{0,3},{1,0},{2,1},{3,2},{4,7},{5,4},{6,5},{7,6},{8,11},{9,8},{10,9... | collective-permute-start | bytes 884744 | tf_op jit(solution)/shard_map/ppermute | solution.py:217
  292.2 147.0 %reduce-scatter.6.cloned.1.call-start = ((), (), s32[]{:S(2)}) async-start(), calls=%async_computation.9 | async-start | bytes 3133440 | tf_op jit(solution)/shard_map/reduce_scatter | solution.py:377
  301.1 14.5 %collective-permute-start.58 = (bf16[128,1152]{1,0:T(8,128)(2,1)S(1)}, bf16[128,1152]{1,0:T(8,128)(2,1)S(1)}, u32[]{:S(2)}, u32[]{:S(2)}) collective-permute-start(bf16[128,1152]{1,0:T(8,128)(2,1)S(1)} %pad_maximum_fusion.32), channel_id=1, source_target_pairs={{0,1},{1,2},{2,3},{3,0},{4,5},{5,6},{6,7},{7,4},{8,9},{9,10},{10,1... | collective-permute-start | bytes 884744 | tf_op jit(solution)/shard_map/ppermute | solution.py:217
  301.8 13.8 %collective-permute-start.59 = (bf16[128,1152]{1,0:T(8,128)(2,1)S(1)}, bf16[128,1152]{1,0:T(8,128)(2,1)S(1)}, u32[]{:S(2)}, u32[]{:S(2)}) collective-permute-start(bf16[128,1152]{1,0:T(8,128)(2,1)S(1)} %pad_maximum_fusion.33), channel_id=1, source_target_pairs={{0,3},{1,0},{2,1},{3,2},{4,7},{5,4},{6,5},{7,6},{8,11},{9,8},{10,9... | collective-permute-start | bytes 884744 | tf_op jit(solution)/shard_map/ppermute | solution.py:217
  340.0 9.5 %collective-permute-start.63 = (bf16[128,1152]{1,0:T(8,128)(2,1)S(1)}, bf16[128,1152]{1,0:T(8,128)(2,1)S(1)}, u32[]{:S(2)}, u32[]{:S(2)}) collective-permute-start(bf16[128,1152]{1,0:T(8,128)(2,1)S(1)} %pad_maximum_fusion.34), channel_id=1, source_target_pairs={{0,1},{1,2},{2,3},{3,0},{4,5},{5,6},{6,7},{7,4},{8,9},{9,10},{10,1... | collective-permute-start | bytes 884744 | tf_op jit(solution)/shard_map/ppermute | solution.py:217
  341.4 8.0 %collective-permute-start.64 = (bf16[128,1152]{1,0:T(8,128)(2,1)S(1)}, bf16[128,1152]{1,0:T(8,128)(2,1)S(1)}, u32[]{:S(2)}, u32[]{:S(2)}) collective-permute-start(bf16[128,1152]{1,0:T(8,128)(2,1)S(1)} %pad_maximum_fusion.35), channel_id=1, source_target_pairs={{0,3},{1,0},{2,1},{3,2},{4,7},{5,4},{6,5},{7,6},{8,11},{9,8},{10,9... | collective-permute-start | bytes 884744 | tf_op jit(solution)/shard_map/ppermute | solution.py:217
  344.8 10.2 %collective-permute-start.67 = (bf16[4,144,1152]{2,1,0:T(8,128)(2,1)S(1)}, bf16[4,144,1152]{2,1,0:T(8,128)(2,1)S(1)}, u32[]{:S(2)}, u32[]{:S(2)}) collective-permute-start(bf16[4,144,1152]{2,1,0:T(8,128)(2,1)S(1)} %broadcast_select_fusion.5), channel_id=1, source_target_pairs={{0,16},{16,0},{1,17},{17,1},{2,18},{18,2},{3,19},{19,3},{4,20},{20... | collective-permute-start | bytes 3981320 | tf_op jit(solution)/shard_map/ppermute | solution.py:20
  350.8 8.8 %collective-permute-start.65 = (bf16[128,1152]{1,0:T(8,128)(2,1)}, bf16[128,1152]{1,0:T(8,128)(2,1)}, u32[]{:S(2)}, u32[]{:S(2)}) collective-permute-start(bf16[128,1152]{1,0:T(8,128)(2,1)} %get-tuple-element.282), channel_id=1, source_target_pairs={{0,1},{1,2},{2,3},{3,0},{4,5},{5,6},{6,7},{7,4},{8,9},{9,10},{10,1... | collective-permute-start | bytes 884744 | tf_op jit(solution)/shard_map/ppermute | solution.py:217
  351.7 7.9 %collective-permute-start.66 = (bf16[128,1152]{1,0:T(8,128)(2,1)}, bf16[128,1152]{1,0:T(8,128)(2,1)}, u32[]{:S(2)}, u32[]{:S(2)}) collective-permute-start(bf16[128,1152]{1,0:T(8,128)(2,1)} %get-tuple-element.282), channel_id=1, source_target_pairs={{0,3},{1,0},{2,1},{3,2},{4,7},{5,4},{6,5},{7,6},{8,11},{9,8},{10,9... | collective-permute-start | bytes 884744 | tf_op jit(solution)/shard_map/ppermute | solution.py:217
  383.9 8.0 %collective-permute-start.71 = (bf16[128,1152]{1,0:T(8,128)(2,1)S(1)}, bf16[128,1152]{1,0:T(8,128)(2,1)S(1)}, u32[]{:S(2)}, u32[]{:S(2)}) collective-permute-start(bf16[128,1152]{1,0:T(8,128)(2,1)S(1)} %pad_maximum_fusion.36), channel_id=1, source_target_pairs={{0,1},{1,2},{2,3},{3,0},{4,5},{5,6},{6,7},{7,4},{8,9},{9,10},{10,1... | collective-permute-start | bytes 884744 | tf_op jit(solution)/shard_map/ppermute | solution.py:217
  395.2 10.6 %collective-permute-start.74 = (bf16[128,1152]{1,0:T(8,128)(2,1)S(1)}, bf16[128,1152]{1,0:T(8,128)(2,1)S(1)}, u32[]{:S(2)}, u32[]{:S(2)}) collective-permute-start(bf16[128,1152]{1,0:T(8,128)(2,1)S(1)} %get-tuple-element.292), channel_id=1, source_target_pairs={{0,1},{1,2},{2,3},{3,0},{4,5},{5,6},{6,7},{7,4},{8,9},{9,10},{10,1... | collective-permute-start | bytes 884744 | tf_op jit(solution)/shard_map/ppermute | solution.py:217
  396.6 9.2 %collective-permute-start.75 = (bf16[128,1152]{1,0:T(8,128)(2,1)S(1)}, bf16[128,1152]{1,0:T(8,128)(2,1)S(1)}, u32[]{:S(2)}, u32[]{:S(2)}) collective-permute-start(bf16[128,1152]{1,0:T(8,128)(2,1)S(1)} %get-tuple-element.292), channel_id=1, source_target_pairs={{0,3},{1,0},{2,1},{3,2},{4,7},{5,4},{6,5},{7,6},{8,11},{9,8},{10,9... | collective-permute-start | bytes 884744 | tf_op jit(solution)/shard_map/ppermute | solution.py:217
  405.9 112.7 %reduce-scatter.8.cloned.1.call-start = ((), (), s32[]{:S(2)}) async-start(), calls=%async_computation.10 | async-start | bytes 1658880 | tf_op jit(solution)/shard_map/reduce_scatter | solution.py:498
  427.6 8.4 %collective-permute-start.79 = (bf16[2,512,512]{2,1,0:T(8,128)(2,1)}, bf16[2,512,512]{2,1,0:T(8,128)(2,1)}, u32[]{:S(2)}, u32[]{:S(2)}) collective-permute-start(bf16[2,512,512]{2,1,0:T(8,128)(2,1)} %get-tuple-element.186), channel_id=1, source_target_pairs={{0,16},{16,0},{1,17},{17,1},{2,18},{18,2},{3,19},{19,3},{4,20},{20... | collective-permute-start | bytes 3145736 | tf_op jit(solution)/shard_map/ppermute | solution.py:20
  452.0 9.4 %collective-permute-start.85 = (bf16[128,1152]{1,0:T(8,128)(2,1)S(1)}, bf16[128,1152]{1,0:T(8,128)(2,1)S(1)}, u32[]{:S(2)}, u32[]{:S(2)}) collective-permute-start(bf16[128,1152]{1,0:T(8,128)(2,1)S(1)} %pad_maximum_fusion.38), channel_id=1, source_target_pairs={{0,1},{1,2},{2,3},{3,0},{4,5},{5,6},{6,7},{7,4},{8,9},{9,10},{10,1... | collective-permute-start | bytes 884744 | tf_op jit(solution)/shard_map/ppermute | solution.py:217
  453.7 7.8 %collective-permute-start.86 = (bf16[128,1152]{1,0:T(8,128)(2,1)S(1)}, bf16[128,1152]{1,0:T(8,128)(2,1)S(1)}, u32[]{:S(2)}, u32[]{:S(2)}) collective-permute-start(bf16[128,1152]{1,0:T(8,128)(2,1)S(1)} %pad_maximum_fusion.39), channel_id=1, source_target_pairs={{0,3},{1,0},{2,1},{3,2},{4,7},{5,4},{6,5},{7,6},{8,11},{9,8},{10,9... | collective-permute-start | bytes 884744 | tf_op jit(solution)/shard_map/ppermute | solution.py:217
  459.0 32.9 %collective-permute-start.82 = (bf16[4,144,1152]{2,1,0:T(8,128)(2,1)}, bf16[4,144,1152]{2,1,0:T(8,128)(2,1)}, u32[]{:S(2)}, u32[]{:S(2)}) collective-permute-start(bf16[4,144,1152]{2,1,0:T(8,128)(2,1)} %broadcast_select_fusion.4), channel_id=1, source_target_pairs={{0,16},{16,0},{1,17},{17,1},{2,18},{18,2},{3,19},{19,3},{4,20},{20... | collective-permute-start | bytes 3981320 | tf_op jit(solution)/shard_map/ppermute | solution.py:20
  465.7 20.5 %all-to-all-start.3 = ((f32[128,8,128]{2,1,0:T(8,128)}), f32[128,8,128]{2,1,0:T(8,128)S(1)}, u32[]{:S(2)}, u32[]{:S(2)}) async-start(f32[128,8,128]{2,1,0:T(8,128)} %pad_maximum_fusion.17), calls=%async_computation.6 | async-start | bytes 1048576 | tf_op jit(solution)/shard_map/all_to_all | solution.py:527
  486.2 26.0 %all-to-all-start.4 = ((bf16[8,272,288]{2,1,0:T(8,128)(2,1)}), bf16[8,272,288]{2,1,0:T(8,128)(2,1)S(1)}, u32[]{:S(2)}, u32[]{:S(2)}) async-start(bf16[8,272,288]{2,1,0:T(8,128)(2,1)} %shard_map.171), calls=%async_computation.7 | async-start | bytes 3342336 | tf_op jit(solution)/shard_map/all_to_all | solution.py:284
  494.3 7.9 %collective-permute-start.83 = (bf16[72,1152]{1,0:T(8,128)(2,1)S(1)}, bf16[72,1152]{1,0:T(8,128)(2,1)S(1)}, u32[]{:S(2)}, u32[]{:S(2)}) collective-permute-start(bf16[72,1152]{1,0:T(8,128)(2,1)S(1)} %get-tuple-element.334), channel_id=1, source_target_pairs={{0,4},{4,8},{8,12},{12,0},{1,5},{5,9},{9,13},{13,1},{2,6},{6,10},{... | collective-permute-start | bytes 497672 | tf_op jit(solution)/shard_map/ppermute | solution.py:217
  502.3 14.4 %collective-permute-start.91 = (bf16[144,1152]{1,0:T(8,128)(2,1)S(1)}, bf16[144,1152]{1,0:T(8,128)(2,1)S(1)}, u32[]{:S(2)}, u32[]{:S(2)}) collective-permute-start(bf16[144,1152]{1,0:T(8,128)(2,1)S(1)} %pad_maximum_fusion.20), channel_id=1, source_target_pairs={{0,4},{4,8},{8,12},{12,0},{1,5},{5,9},{9,13},{13,1},{2,6},{6,10},{... | collective-permute-start | bytes 995336 | tf_op jit(solution)/shard_map/ppermute | solution.py:217
  502.6 14.8 %collective-permute-start.92 = (bf16[144,1152]{1,0:T(8,128)(2,1)S(1)}, bf16[144,1152]{1,0:T(8,128)(2,1)S(1)}, u32[]{:S(2)}, u32[]{:S(2)}) collective-permute-start(bf16[144,1152]{1,0:T(8,128)(2,1)S(1)} %pad_maximum_fusion.21), channel_id=1, source_target_pairs={{0,12},{4,0},{8,4},{12,8},{1,13},{5,1},{9,5},{13,9},{2,14},{6,2},{... | collective-permute-start | bytes 995336 | tf_op jit(solution)/shard_map/ppermute | solution.py:217
  514.9 14.1 %collective-permute-start.87 = (bf16[64,1152]{1,0:T(8,128)(2,1)S(1)}, bf16[64,1152]{1,0:T(8,128)(2,1)S(1)}, u32[]{:S(2)}, u32[]{:S(2)}) collective-permute-start(bf16[64,1152]{1,0:T(8,128)(2,1)S(1)} %copy-done.124), channel_id=1, source_target_pairs={{12,0},{8,4},{28,8},{24,12},{76,16},{72,20},{92,24},{88,28},{4,64}... | collective-permute-start | bytes 442376 | tf_op jit(solution)/shard_map/ppermute | solution.py:514
  515.3 13.8 %collective-permute-start.88 = (bf16[64,1152]{1,0:T(8,128)(2,1)S(1)}, bf16[64,1152]{1,0:T(8,128)(2,1)S(1)}, u32[]{:S(2)}, u32[]{:S(2)}) collective-permute-start(bf16[64,1152]{1,0:T(8,128)(2,1)S(1)} %copy-done.123), channel_id=1, source_target_pairs={{8,0},{12,4},{24,8},{28,12},{72,16},{76,20},{88,24},{92,28},{0,64}... | collective-permute-start | bytes 442376 | tf_op jit(solution)/shard_map/ppermute | solution.py:514
  515.3 13.8 %collective-permute-start.89 = (bf16[64,1152]{1,0:T(8,128)(2,1)S(1)}, bf16[64,1152]{1,0:T(8,128)(2,1)S(1)}, u32[]{:S(2)}, u32[]{:S(2)}) collective-permute-start(bf16[64,1152]{1,0:T(8,128)(2,1)S(1)} %copy-done.122), channel_id=1, source_target_pairs={{4,0},{0,4},{20,8},{16,12},{68,16},{64,20},{84,24},{80,28},{12,64}... | collective-permute-start | bytes 442376 | tf_op jit(solution)/shard_map/ppermute | solution.py:514
  516.7 12.3 %collective-permute-start.90 = (bf16[64,1152]{1,0:T(8,128)(2,1)S(1)}, bf16[64,1152]{1,0:T(8,128)(2,1)S(1)}, u32[]{:S(2)}, u32[]{:S(2)}) collective-permute-start(bf16[64,1152]{1,0:T(8,128)(2,1)S(1)} %copy-done.121), channel_id=1, source_target_pairs={{0,0},{4,4},{16,8},{20,12},{64,16},{68,20},{80,24},{84,28},{8,64},... | collective-permute-start | bytes 442376 | tf_op jit(solution)/shard_map/ppermute | solution.py:514
  520.7 22.2 %all-to-all-start.2 = ((bf16[8,144,288]{2,1,0:T(8,128)(2,1)}), bf16[8,144,288]{2,1,0:T(8,128)(2,1)S(1)}, u32[]{:S(2)}, u32[]{:S(2)}) async-start(bf16[8,144,288]{2,1,0:T(8,128)(2,1)} %shard_map.169), calls=%async_computation.5 | async-start | bytes 1769472 | tf_op jit(solution)/shard_map/all_to_all | solution.py:284
  (221 other events, 1306.6 us)
Sparse Core Ops, SparseCore 0:
  48.1 30.3 all-gather.6
  84.0 35.8 all-gather.8
  127.4 44.1 all-gather.10
  292.3 32.2 reduce-scatter.3
  406.0 33.1 reduce-scatter.5
  441.5 24.2 reduce-scatter.7

commit v2 on v1

--- a/solution.py
+++ b/solution.py
@@ -388,6 +388,7 @@
     grad_w_query = dot("nf,nd->fd", grad_query, rows1).astype(BF)
     from_query = dot("nf,fd->nd", grad_query, w_query)
     sent, part_mlp, grad_w_out, grad_w_query, from_query = tie(sent, part_mlp, grad_w_out, grad_w_query, from_query)
+    part_mlp = to_owner(part_mlp)
     pair = grad_own + sent.astype(F32)
     sum_value = jnp.sum(pair[1], axis=0)
     pair = pair.astype(BF)
@@ -404,11 +405,10 @@
         second = jnp.concatenate([heads(grad_w_value), heads(grad_w_out)], axis=1)
         return pick(on_first, second, first), pick(on_first, first, second)
 
-    passed, pair, part_mlp = tie(collect_far(chunks), pair, part_mlp)
+    passed, pair = tie(collect_far(chunks), pair)
     given, kept = attn_grads(pair)
-    part_mlp = to_owner(part_mlp)
     part_attn = (kept.astype(F32) + swap(given, "c").astype(F32)).astype(BF)
-    ga1, gain1, offset1 = tie(collect_near(chunks, passed), gain1, offset1)
+    ga1, gain1, offset1, part_mlp = tie(collect_near(chunks, passed), gain1, offset1, part_mlp)
     grad_hidden = norm_back(grad_middle, ga1, unit1, rstd1, vectors[0])[0]
     grad_vectors = [gain1, gain2, offset1, jnp.sum(grad_middle, axis=0), offset2, jnp.sum(grad_out, axis=0)]
     grad_b_up = jnp.sum(grad_pre, axis=0)
@@ -508,8 +508,7 @@
     half = rows
     out_grad, out_result = grad0.astype(BF), result.astype(BF)
     blocks = by_xor([out_grad[:half], out_grad[half:], out_result[:half], out_result[half:]], own_y)
-    passed, blocks = tie(collect_far(chunks, "y"), blocks)
-    attn0 = collect_near(chunks, passed, "y")
+    attn0, blocks = tie(collect_near(chunks, collect_far(chunks, "y"), "y"), blocks)
     blocks = [
         lax.ppermute(block, ("xl", "c", "y"), [(b, a) for a, b in route]) for block, route in zip(blocks, routes)
     ]
@@ -524,9 +523,9 @@
     grad_bias = jnp.where(here, grad_bias[:, None, :, None], 0.0)
     grad_bias = jnp.broadcast_to(grad_bias, (2, 4, 4, 4, lines - 1, LANES)).reshape(128, lines - 1, LANES)
     sent = jnp.concatenate([pack_vectors(grad_vectors).reshape(128, 1, LANES), grad_bias], axis=1)
+
+    grad_attn, sent = tie(to_owners((attn0, attn1)), sent)
     owned = lax.all_to_all(sent, AXES, 0, 0)
-
-    grad_attn = to_owners((attn0, attn1))
     owned = jnp.sum(owned, axis=0)
     share_vec = owned[0, : 6 * piece].reshape(6, piece)
     share_qv = owned[1:3, :hd]

time: 562 us -> 556 us (0.989)
  waiting for transfers between devices: 149 us -> 140 us
    all_to_all x2, waiting for transfers between devices: 19.3 us -> 2.91 us  [to_owners(): arrived = lax.all_to_all(chunks, ('xl', 'xh', 'c'), 0, 0)]
    ppermute x68, waiting for transfers between devices: 102 us -> 110 us  [ring(): return lax.ppermute(value, axis, [(i, (i + step) % 4) for i in range(4)])]
  transfers between devices with their start and end apart: 104 -> 104, of which waited for: 47 -> 48; matrix products, arithmetic and copies ran while one was open for 21% -> 21% of each run, Pallas kernels for 8% -> 8%
where the time goes in v2:
time: 556 us; the launch traced here: 545 us
  starting transfers between devices  170 us (31%)
  waiting for transfers between devices  140 us (25%)
  local copies, waits for them, and re-layouts  62.5 us (11%)
  other arithmetic  56.6 us (10%)
  matrix products  52.2 us (9%)
  Pallas kernels  46.1 us (8%)
  between operations  17.9 us (3%)
    ppermute x68, starting transfers between devices, ring(): return lax.ppermute(value, axis, [(i, (i + step) % 4) for i in range(4)])  116 us
    ppermute x68, waiting for transfers between devices, ring(): return lax.ppermute(value, axis, [(i, (i + step) % 4) for i in range(4)])  110 us
    dot_general x28, matrix products, dot(): return jnp.einsum(spec, left, right, preferred_element_type=F32)  52.2 us
    pallas_call x12, Pallas kernels, on_vmem(): pl.pallas_call(kernel, in_specs=[pl.BlockSpec(memory_space=pltpu.SMEM)] *...  46.1 us
    unnamed x392, local copies, waits for them, and re-layouts  28.7 us
    all_to_all x1, starting transfers between devices, body(): owned = lax.all_to_all(sent, AXES, 0, 0)  11.5 us
  transfers between devices with their start and end apart: 104, of which 48 were waited for; matrix products, arithmetic and copies ran while one was open for 21% of the time, Pallas kernels for 8%

profile of v2, /device:TPU:0, one launch (start us, length us, event | category | flops | bytes accessed | tf_op | source)
XLA Modules:
  0.0 545.3 jit_solution(12236420584888332761)
XLA Ops:
  10.0 3.2 collective-permute-start
  16.1 8.1 %all-to-all-start = ((bf16[8,144,288]{2,1,0:T(8,128)(2,1)}), bf16[8,144,288]{2,1,0:T(8,128)(2,1)}, u32[]{:S(2)}, u32[]{:S(2)}) async-start(bf16[8,144,288]{2,1,0:T(8,128)(2,1)} %bitcast.19), calls=%async_computation | async-start | bytes 1769472 | tf_op jit(solution)/shard_map/all_to_all | solution.py:276
  30.6 7.5 %collective-permute-done.4 = bf16[128,1152]{1,0:T(8,128)(2,1)S(1)} collective-permute-done((bf16[128,1152]{1,0:T(8,128)(2,1)S(1)}, bf16[128,1152]{1,0:T(8,128)(2,1)S(1)}, u32[]{:S(2)}, u32[]{:S(2)}) %collective-permute-start.4) | collective-permute-done | bytes 294944 | tf_op jit(solution)/shard_map/ppermute | solution.py:217
  39.6 3.2 collective-permute-start.7
  55.5 8.1 %all-to-all-start.1 = ((f32[128,8,128]{2,1,0:T(8,128)}), f32[128,8,128]{2,1,0:T(8,128)}, u32[]{:S(2)}, u32[]{:S(2)}) async-start(f32[128,8,128]{2,1,0:T(8,128)} %broadcast_in_dim.47), calls=%async_computation.1 | async-start | bytes 1048576 | tf_op jit(solution)/shard_map/all_to_all | solution.py:454
  68.5 2.4 collective-permute-start.12
  71.9 3.0 collective-permute-done.11
  96.6 4.2 shard_map.161
  107.3 3.3 collective-permute-done.17
  110.6 9.3 %all-gather.9.cloned.1.call-done = bf16[1088,1152]{1,0:T(8,128)(2,1)} async-done(((bf16[272,1152]{1,0:T(8,128)(2,1)}), bf16[1088,1152]{1,0:T(8,128)(2,1)}) %all-gather.9.cloned.1.call-update) | async-done | bytes 2506768 | tf_op jit(solution)/shard_map/all_gather | solution.py:458
  127.4 5.0 collective-permute-done.19
  140.9 4.4 collective-permute-done.22
  148.7 3.0 collective-permute-done.24
  151.7 3.5 multiply_convert_fusion.1
  160.6 3.0 collective-permute-done.26
  167.3 4.6 collective-permute-done.27
  179.2 7.3 %collective-permute-done.30 = bf16[128,1152]{1,0:T(8,128)(2,1)S(1)} collective-permute-done((bf16[128,1152]{1,0:T(8,128)(2,1)S(1)}, bf16[128,1152]{1,0:T(8,128)(2,1)S(1)}, u32[]{:S(2)}, u32[]{:S(2)}) %collective-permute-start.30) | collective-permute-done | bytes 294944 | tf_op jit(solution)/shard_map/ppermute | solution.py:217
  200.7 4.2 shard_map.162
  206.9 3.1 collective-permute-start.39
  215.7 3.0 collective-permute-start.41
  218.8 7.2 %collective-permute-done.40 = bf16[128,1152]{1,0:T(8,128)(2,1)S(1)} collective-permute-done((bf16[128,1152]{1,0:T(8,128)(2,1)S(1)}, bf16[128,1152]{1,0:T(8,128)(2,1)S(1)}, u32[]{:S(2)}, u32[]{:S(2)}) %collective-permute-start.40) | collective-permute-done | bytes 294944 | tf_op jit(solution)/shard_map/ppermute | solution.py:217
  232.7 6.1 %collective-permute-done.43 = bf16[128,1152]{1,0:T(8,128)(2,1)S(1)} collective-permute-done((bf16[128,1152]{1,0:T(8,128)(2,1)S(1)}, bf16[128,1152]{1,0:T(8,128)(2,1)S(1)}, u32[]{:S(2)}, u32[]{:S(2)}) %collective-permute-start.43) | collective-permute-done | bytes 294944 | tf_op jit(solution)/shard_map/ppermute | solution.py:217
  240.2 2.5 collective-permute-start.46
  245.9 3.8 fusion.95
  262.4 3.1 collective-permute-done.49
  273.4 2.3 shard_map.163
  283.3 4.0 shard_map.164
  287.4 3.3 collective-permute-done.53
  293.7 2.8 collective-permute-start.57
  296.6 3.3 collective-permute-done.56
  301.8 2.7 collective-permute-start.59
  307.3 8.3 %shard_map.165 = (bf16[512,512]{1,0:T(8,128)(2,1)S(1)}, f32[1,512]{1,0:T(1,128)S(1)}, f32[2,512,512]{2,1,0:T(8,128)S(1)}, bf16[2,512,512]{2,1,0:T(8,128)(2,1)S(1)}) custom-call(bf16[512,512]{1,0:T(8,128)(2,1)S(1)} %copy-done.17, bf16[512,1024]{1,0:T(8,128)(2,1)S(1)} %copy-done.11, bf16[512,1024]{1,0:T(8,128)(2,1)S(1)} %copy-done.13, ...), custom_call_target="tpu_custom_call" | custom-call | flops 1048576 | bytes 65536 | tf_op jit(solution)/shard_map/pallas_call | solution.py:95
  322.0 2.3 fusion.113
  324.6 3.1 fusion.98
  335.1 3.7 collective-permute-done.61
  344.9 4.5 collective-permute-done.63
  351.1 2.3 collective-permute-start.66
  355.0 3.7 collective-permute-done.65
  362.6 2.8 collective-permute-start.69
  368.3 4.5 fusion.93
  378.3 3.9 collective-permute-done.70
  386.5 2.4 shard_map.166
  396.6 3.9 shard_map.167
  400.5 3.5 collective-permute-done.74
  407.3 2.4 collective-permute-start.78
  414.2 2.3 convolution_convert_fusion.14.grad
  416.6 9.3 %shard_map.168 = (bf16[512,512]{1,0:T(8,128)(2,1)S(1)}, f32[1,512]{1,0:T(1,128)S(1)}, f32[2,512,512]{2,1,0:T(8,128)S(1)}, bf16[2,512,512]{2,1,0:T(8,128)(2,1)}) custom-call(bf16[512,512]{1,0:T(8,128)(2,1)S(1)} %copy-done.15, bf16[512,1024]{1,0:T(8,128)(2,1)S(1)} %copy-done.7, bf16[512,1024]{1,0:T(8,128)(2,1)S(1)} %copy-done.9, ...), custom_call_target="tpu_custom_call" | custom-call | flops 1048576 | bytes 65536 | tf_op jit(solution)/shard_map/pallas_call | solution.py:95
  426.3 3.4 convolution_convert_fusion.3
  431.8 2.3 fusion.114
  434.1 3.3 reduce-scatter.6.cloned.1.call-done
  441.3 4.5 all-to-all-start.2
  455.2 3.9 collective-permute-done.80
  466.4 2.8 collective-permute-done.87
  470.2 2.8 convert_reduce_fusion
  475.5 3.1 collective-permute-start.85
  478.9 3.0 collective-permute-done.83
  482.4 3.0 collective-permute-start.86
  486.2 4.6 collective-permute-done.84
  493.1 4.2 all-to-all-start.3
  500.0 2.8 shard_map.171
  503.8 3.0 collective-permute-start.89
  508.3 2.9 all-to-all-done.3
  511.3 11.5 %all-to-all-start.4 = ((f32[128,8,128]{2,1,0:T(8,128)}), f32[128,8,128]{2,1,0:T(8,128)S(1)}, u32[]{:S(2)}, u32[]{:S(2)}) async-start(f32[128,8,128]{2,1,0:T(8,128)} %pad_maximum_fusion.17), calls=%async_computation.7 | async-start | bytes 1048576 | tf_op jit(solution)/shard_map/all_to_all | solution.py:528
  525.3 10.0 %all-to-all-done.4 = f32[128,8,128]{2,1,0:T(8,128)S(1)} async-done(((f32[128,8,128]{2,1,0:T(8,128)}), f32[128,8,128]{2,1,0:T(8,128)S(1)}, u32[]{:S(2)}, u32[]{:S(2)}) %all-to-all-start.4) | async-done | bytes 524320 | tf_op jit(solution)/shard_map/all_to_all | solution.py:528
  (822 shorter events, 258.8 us)
Async XLA Ops:
  10.0 14.7 %collective-permute-start = (bf16[64,1152]{1,0:T(8,128)(2,1)S(1)}, bf16[64,1152]{1,0:T(8,128)(2,1)S(1)}, u32[]{:S(2)}, u32[]{:S(2)}) collective-permute-start(bf16[64,1152]{1,0:T(8,128)(2,1)S(1)} %get-tuple-element.417), channel_id=1, source_target_pairs={{0,12},{4,8},{8,28},{12,24},{16,76},{20,72},{24,92},{28,88},{64,4}... | collective-permute-start | bytes 442376 | tf_op jit(solution)/shard_map/ppermute | solution.py:439
  13.2 11.6 %collective-permute-start.1 = (bf16[64,1152]{1,0:T(8,128)(2,1)S(1)}, bf16[64,1152]{1,0:T(8,128)(2,1)S(1)}, u32[]{:S(2)}, u32[]{:S(2)}) collective-permute-start(bf16[64,1152]{1,0:T(8,128)(2,1)S(1)} %get-tuple-element.414), channel_id=1, source_target_pairs={{0,8},{4,12},{8,24},{12,28},{16,72},{20,76},{24,88},{28,92},{64,0}... | collective-permute-start | bytes 442376 | tf_op jit(solution)/shard_map/ppermute | solution.py:439
  14.1 10.7 %collective-permute-start.2 = (bf16[64,1152]{1,0:T(8,128)(2,1)S(1)}, bf16[64,1152]{1,0:T(8,128)(2,1)S(1)}, u32[]{:S(2)}, u32[]{:S(2)}) collective-permute-start(bf16[64,1152]{1,0:T(8,128)(2,1)S(1)} %get-tuple-element.415), channel_id=1, source_target_pairs={{0,4},{4,0},{8,20},{12,16},{16,68},{20,64},{24,84},{28,80},{64,12}... | collective-permute-start | bytes 442376 | tf_op jit(solution)/shard_map/ppermute | solution.py:439
  14.3 10.5 %collective-permute-start.3 = (bf16[64,1152]{1,0:T(8,128)(2,1)S(1)}, bf16[64,1152]{1,0:T(8,128)(2,1)S(1)}, u32[]{:S(2)}, u32[]{:S(2)}) collective-permute-start(bf16[64,1152]{1,0:T(8,128)(2,1)S(1)} %get-tuple-element.416), channel_id=1, source_target_pairs={{0,0},{4,4},{8,16},{12,20},{16,64},{20,68},{24,80},{28,84},{64,8},... | collective-permute-start | bytes 442376 | tf_op jit(solution)/shard_map/ppermute | solution.py:439
  16.1 26.7 %all-to-all-start = ((bf16[8,144,288]{2,1,0:T(8,128)(2,1)}), bf16[8,144,288]{2,1,0:T(8,128)(2,1)}, u32[]{:S(2)}, u32[]{:S(2)}) async-start(bf16[8,144,288]{2,1,0:T(8,128)(2,1)} %bitcast.19), calls=%async_computation | async-start | bytes 1769472 | tf_op jit(solution)/shard_map/all_to_all | solution.py:276
  24.2 54.4 %all-gather.7.cloned.1.call-start = ((), (), s32[]{:S(2)}) async-start(), calls=%async_computation.11 | async-start | bytes 1658880 | tf_op jit(solution)/shard_map/all_gather | solution.py:453
  26.4 11.7 %collective-permute-start.4 = (bf16[128,1152]{1,0:T(8,128)(2,1)S(1)}, bf16[128,1152]{1,0:T(8,128)(2,1)S(1)}, u32[]{:S(2)}, u32[]{:S(2)}) collective-permute-start(bf16[128,1152]{1,0:T(8,128)(2,1)S(1)} %pad_maximum_fusion.22), channel_id=1, source_target_pairs={{0,1},{1,2},{2,3},{3,0},{4,5},{5,6},{6,7},{7,4},{8,9},{9,10},{10,1... | collective-permute-start | bytes 884744 | tf_op jit(solution)/shard_map/ppermute | solution.py:217
  28.4 10.5 %collective-permute-start.5 = (bf16[128,1152]{1,0:T(8,128)(2,1)S(1)}, bf16[128,1152]{1,0:T(8,128)(2,1)S(1)}, u32[]{:S(2)}, u32[]{:S(2)}) collective-permute-start(bf16[128,1152]{1,0:T(8,128)(2,1)S(1)} %pad_maximum_fusion.22), channel_id=1, source_target_pairs={{0,3},{1,0},{2,1},{3,2},{4,7},{5,4},{6,5},{7,6},{8,11},{9,8},{10,9... | collective-permute-start | bytes 884744 | tf_op jit(solution)/shard_map/ppermute | solution.py:217
  38.8 26.8 %collective-permute-start.6 = (bf16[64,1152]{1,0:T(8,128)(2,1)}, bf16[64,1152]{1,0:T(8,128)(2,1)}, u32[]{:S(2)}, u32[]{:S(2)}) collective-permute-start(bf16[64,1152]{1,0:T(8,128)(2,1)} %slice.782), channel_id=1, source_target_pairs={{0,1},{1,2},{2,3},{3,0},{4,5},{5,6},{6,7},{7,4},{8,9},{9,10},{10,1... | collective-permute-start | bytes 442376 | tf_op jit(solution)/shard_map/ppermute | solution.py:217
  39.6 31.4 %collective-permute-start.7 = (bf16[64,1152]{1,0:T(8,128)(2,1)}, bf16[64,1152]{1,0:T(8,128)(2,1)}, u32[]{:S(2)}, u32[]{:S(2)}) collective-permute-start(bf16[64,1152]{1,0:T(8,128)(2,1)} %slice.783), channel_id=1, source_target_pairs={{0,3},{1,0},{2,1},{3,2},{4,7},{5,4},{6,5},{7,6},{8,11},{9,8},{10,9... | collective-permute-start | bytes 442376 | tf_op jit(solution)/shard_map/ppermute | solution.py:217
  50.4 16.2 %collective-permute-start.10 = (bf16[272,576]{1,0:T(8,128)(2,1)}, bf16[272,576]{1,0:T(8,128)(2,1)S(1)}, u32[]{:S(2)}, u32[]{:S(2)}) collective-permute-start(bf16[272,576]{1,0:T(8,128)(2,1)} %pad_maximum_fusion.19), channel_id=1, source_target_pairs={{0,64},{64,32},{32,96},{96,0},{1,65},{65,33},{33,97},{97,1},{2,66}... | collective-permute-start | bytes 940040 | tf_op jit(solution)/shard_map/ppermute | solution.py:319
  52.1 15.5 %collective-permute-start.9 = (bf16[272,576]{1,0:T(8,128)(2,1)}, bf16[272,576]{1,0:T(8,128)(2,1)}, u32[]{:S(2)}, u32[]{:S(2)}) collective-permute-start(bf16[272,576]{1,0:T(8,128)(2,1)} %pad_maximum_fusion.19), channel_id=1, source_target_pairs={{64,0},{32,64},{96,32},{0,96},{65,1},{33,65},{97,33},{1,97},{66,2}... | collective-permute-start | bytes 940040 | tf_op jit(solution)/shard_map/ppermute | solution.py:319
  55.5 23.8 %all-to-all-start.1 = ((f32[128,8,128]{2,1,0:T(8,128)}), f32[128,8,128]{2,1,0:T(8,128)}, u32[]{:S(2)}, u32[]{:S(2)}) async-start(f32[128,8,128]{2,1,0:T(8,128)} %broadcast_in_dim.47), calls=%async_computation.1 | async-start | bytes 1048576 | tf_op jit(solution)/shard_map/all_to_all | solution.py:454
  63.5 56.3 %all-gather.9.cloned.1.call-start = ((), (), s32[]{:S(2)}) async-start(), calls=%async_computation.12 | async-start | bytes 3133440 | tf_op jit(solution)/shard_map/all_gather | solution.py:458
  66.6 8.2 %collective-permute-start.11 = (bf16[136,576]{1,0:T(8,128)(2,1)S(1)}, bf16[136,576]{1,0:T(8,128)(2,1)S(1)}, u32[]{:S(2)}, u32[]{:S(2)}) collective-permute-start(bf16[136,576]{1,0:T(8,128)(2,1)S(1)} %slice.791), channel_id=1, source_target_pairs={{0,64},{64,32},{32,96},{96,0},{1,65},{65,33},{33,97},{97,1},{2,66}... | collective-permute-start | bytes 470024 | tf_op jit(solution)/shard_map/ppermute | solution.py:321
  83.8 89.7 %all-gather.11.cloned.1.call-start = ((), (), s32[]{:S(2)}) async-start(), calls=%async_computation.13 | async-start | bytes 4792320 | tf_op jit(solution)/shard_map/all_gather | solution.py:473
  91.2 10.7 %collective-permute-start.15 = (bf16[128,1152]{1,0:T(8,128)(2,1)S(1)}, bf16[128,1152]{1,0:T(8,128)(2,1)S(1)}, u32[]{:S(2)}, u32[]{:S(2)}) collective-permute-start(bf16[128,1152]{1,0:T(8,128)(2,1)S(1)} %pad_maximum_fusion.23), channel_id=1, source_target_pairs={{0,1},{1,2},{2,3},{3,0},{4,5},{5,6},{6,7},{7,4},{8,9},{9,10},{10,1... | collective-permute-start | bytes 884744 | tf_op jit(solution)/shard_map/ppermute | solution.py:217
  92.9 9.0 %collective-permute-start.16 = (bf16[128,1152]{1,0:T(8,128)(2,1)S(1)}, bf16[128,1152]{1,0:T(8,128)(2,1)S(1)}, u32[]{:S(2)}, u32[]{:S(2)}) collective-permute-start(bf16[128,1152]{1,0:T(8,128)(2,1)S(1)} %pad_maximum_fusion.23), channel_id=1, source_target_pairs={{0,3},{1,0},{2,1},{3,2},{4,7},{5,4},{6,5},{7,6},{8,11},{9,8},{10,9... | collective-permute-start | bytes 884744 | tf_op jit(solution)/shard_map/ppermute | solution.py:217
  119.9 13.8 %collective-permute-start.21 = (bf16[4,272,1152]{2,1,0:T(8,128)(2,1)}, bf16[4,272,1152]{2,1,0:T(8,128)(2,1)}, u32[]{:S(2)}, u32[]{:S(2)}) collective-permute-start(bf16[4,272,1152]{2,1,0:T(8,128)(2,1)} %bitcast.257), channel_id=1, source_target_pairs={{0,16},{16,0},{1,17},{17,1},{2,18},{18,2},{3,19},{19,3},{4,20},{20... | collective-permute-start | bytes 7520264 | tf_op jit(solution)/shard_map/ppermute | solution.py:20
  121.6 10.8 %collective-permute-start.19 = (bf16[128,1152]{1,0:T(8,128)(2,1)S(1)}, bf16[128,1152]{1,0:T(8,128)(2,1)}, u32[]{:S(2)}, u32[]{:S(2)}) collective-permute-start(bf16[128,1152]{1,0:T(8,128)(2,1)S(1)} %pad_maximum_fusion.24), channel_id=1, source_target_pairs={{0,1},{1,2},{2,3},{3,0},{4,5},{5,6},{6,7},{7,4},{8,9},{9,10},{10,1... | collective-permute-start | bytes 884744 | tf_op jit(solution)/shard_map/ppermute | solution.py:217
  123.2 9.2 %collective-permute-start.20 = (bf16[128,1152]{1,0:T(8,128)(2,1)S(1)}, bf16[128,1152]{1,0:T(8,128)(2,1)S(1)}, u32[]{:S(2)}, u32[]{:S(2)}) collective-permute-start(bf16[128,1152]{1,0:T(8,128)(2,1)S(1)} %pad_maximum_fusion.25), channel_id=1, source_target_pairs={{0,3},{1,0},{2,1},{3,2},{4,7},{5,4},{6,5},{7,6},{8,11},{9,8},{10,9... | collective-permute-start | bytes 884744 | tf_op jit(solution)/shard_map/ppermute | solution.py:217
  127.3 197.3 %reduce-scatter.4.cloned.1.call-start = ((), (), s32[]{:S(2)}) async-start(), calls=%async_computation.8 | async-start | bytes 3133440 | tf_op jit(solution)/shard_map/reduce_scatter | solution.py:377
  135.3 9.9 %collective-permute-start.22 = (bf16[128,1152]{1,0:T(8,128)(2,1)S(1)}, bf16[128,1152]{1,0:T(8,128)(2,1)S(1)}, u32[]{:S(2)}, u32[]{:S(2)}) collective-permute-start(bf16[128,1152]{1,0:T(8,128)(2,1)S(1)} %get-tuple-element.310), channel_id=1, source_target_pairs={{0,1},{1,2},{2,3},{3,0},{4,5},{5,6},{6,7},{7,4},{8,9},{9,10},{10,1... | collective-permute-start | bytes 884744 | tf_op jit(solution)/shard_map/ppermute | solution.py:217
  137.0 8.2 %collective-permute-start.23 = (bf16[128,1152]{1,0:T(8,128)(2,1)S(1)}, bf16[128,1152]{1,0:T(8,128)(2,1)S(1)}, u32[]{:S(2)}, u32[]{:S(2)}) collective-permute-start(bf16[128,1152]{1,0:T(8,128)(2,1)S(1)} %get-tuple-element.310), channel_id=1, source_target_pairs={{0,3},{1,0},{2,1},{3,2},{4,7},{5,4},{6,5},{7,6},{8,11},{9,8},{10,9... | collective-permute-start | bytes 884744 | tf_op jit(solution)/shard_map/ppermute | solution.py:217
  163.9 8.0 %collective-permute-start.27 = (bf16[128,1152]{1,0:T(8,128)(2,1)S(1)}, bf16[128,1152]{1,0:T(8,128)(2,1)S(1)}, u32[]{:S(2)}, u32[]{:S(2)}) collective-permute-start(bf16[128,1152]{1,0:T(8,128)(2,1)S(1)} %pad_maximum_fusion.26), channel_id=1, source_target_pairs={{0,1},{1,2},{2,3},{3,0},{4,5},{5,6},{6,7},{7,4},{8,9},{9,10},{10,1... | collective-permute-start | bytes 884744 | tf_op jit(solution)/shard_map/ppermute | solution.py:217
  175.1 11.4 %collective-permute-start.32 = (bf16[4,144,1152]{2,1,0:T(8,128)(2,1)S(1)}, bf16[4,144,1152]{2,1,0:T(8,128)(2,1)S(1)}, u32[]{:S(2)}, u32[]{:S(2)}) collective-permute-start(bf16[4,144,1152]{2,1,0:T(8,128)(2,1)S(1)} %slice.670), channel_id=1, source_target_pairs={{0,16},{16,0},{1,17},{17,1},{2,18},{18,2},{3,19},{19,3},{4,20},{20... | collective-permute-start | bytes 3981320 | tf_op jit(solution)/shard_map/ppermute | solution.py:20
  175.9 10.6 %collective-permute-start.30 = (bf16[128,1152]{1,0:T(8,128)(2,1)S(1)}, bf16[128,1152]{1,0:T(8,128)(2,1)S(1)}, u32[]{:S(2)}, u32[]{:S(2)}) collective-permute-start(bf16[128,1152]{1,0:T(8,128)(2,1)S(1)} %get-tuple-element.296), channel_id=1, source_target_pairs={{0,1},{1,2},{2,3},{3,0},{4,5},{5,6},{6,7},{7,4},{8,9},{9,10},{10,1... | collective-permute-start | bytes 884744 | tf_op jit(solution)/shard_map/ppermute | solution.py:217
  177.4 9.1 %collective-permute-start.31 = (bf16[128,1152]{1,0:T(8,128)(2,1)S(1)}, bf16[128,1152]{1,0:T(8,128)(2,1)S(1)}, u32[]{:S(2)}, u32[]{:S(2)}) collective-permute-start(bf16[128,1152]{1,0:T(8,128)(2,1)S(1)} %get-tuple-element.296), channel_id=1, source_target_pairs={{0,3},{1,0},{2,1},{3,2},{4,7},{5,4},{6,5},{7,6},{8,11},{9,8},{10,9... | collective-permute-start | bytes 884744 | tf_op jit(solution)/shard_map/ppermute | solution.py:217
  195.9 9.0 %collective-permute-start.36 = (bf16[64,1152]{1,0:T(8,128)(2,1)S(1)}, bf16[64,1152]{1,0:T(8,128)(2,1)S(1)}, u32[]{:S(2)}, u32[]{:S(2)}) collective-permute-start(bf16[64,1152]{1,0:T(8,128)(2,1)S(1)} %slice.680), channel_id=1, source_target_pairs={{0,1},{1,2},{2,3},{3,0},{4,5},{5,6},{6,7},{7,4},{8,9},{9,10},{10,1... | collective-permute-start | bytes 442376 | tf_op jit(solution)/shard_map/ppermute | solution.py:217
  197.3 7.6 %collective-permute-start.37 = (bf16[64,1152]{1,0:T(8,128)(2,1)S(1)}, bf16[64,1152]{1,0:T(8,128)(2,1)S(1)}, u32[]{:S(2)}, u32[]{:S(2)}) collective-permute-start(bf16[64,1152]{1,0:T(8,128)(2,1)S(1)} %slice.681), channel_id=1, source_target_pairs={{0,3},{1,0},{2,1},{3,2},{4,7},{5,4},{6,5},{7,6},{8,11},{9,8},{10,9... | collective-permute-start | bytes 442376 | tf_op jit(solution)/shard_map/ppermute | solution.py:217
  214.0 13.1 %collective-permute-start.42 = (bf16[4,272,1152]{2,1,0:T(8,128)(2,1)S(1)}, bf16[4,272,1152]{2,1,0:T(8,128)(2,1)S(1)}, u32[]{:S(2)}, u32[]{:S(2)}) collective-permute-start(bf16[4,272,1152]{2,1,0:T(8,128)(2,1)S(1)} %slice.687), channel_id=1, source_target_pairs={{0,16},{16,0},{1,17},{17,1},{2,18},{18,2},{3,19},{19,3},{4,20},{20... | collective-permute-start | bytes 7520264 | tf_op jit(solution)/shard_map/ppermute | solution.py:20
  215.4 10.7 %collective-permute-start.40 = (bf16[128,1152]{1,0:T(8,128)(2,1)S(1)}, bf16[128,1152]{1,0:T(8,128)(2,1)S(1)}, u32[]{:S(2)}, u32[]{:S(2)}) collective-permute-start(bf16[128,1152]{1,0:T(8,128)(2,1)S(1)} %pad_maximum_fusion.28), channel_id=1, source_target_pairs={{0,1},{1,2},{2,3},{3,0},{4,5},{5,6},{6,7},{7,4},{8,9},{9,10},{10,1... | collective-permute-start | bytes 884744 | tf_op jit(solution)/shard_map/ppermute | solution.py:217
  215.7 10.3 %collective-permute-start.41 = (bf16[128,1152]{1,0:T(8,128)(2,1)S(1)}, bf16[128,1152]{1,0:T(8,128)(2,1)S(1)}, u32[]{:S(2)}, u32[]{:S(2)}) collective-permute-start(bf16[128,1152]{1,0:T(8,128)(2,1)S(1)} %pad_maximum_fusion.29), channel_id=1, source_target_pairs={{0,3},{1,0},{2,1},{3,2},{4,7},{5,4},{6,5},{7,6},{8,11},{9,8},{10,9... | collective-permute-start | bytes 884744 | tf_op jit(solution)/shard_map/ppermute | solution.py:217
  229.0 9.9 %collective-permute-start.43 = (bf16[128,1152]{1,0:T(8,128)(2,1)S(1)}, bf16[128,1152]{1,0:T(8,128)(2,1)S(1)}, u32[]{:S(2)}, u32[]{:S(2)}) collective-permute-start(bf16[128,1152]{1,0:T(8,128)(2,1)S(1)} %get-tuple-element.306), channel_id=1, source_target_pairs={{0,1},{1,2},{2,3},{3,0},{4,5},{5,6},{6,7},{7,4},{8,9},{9,10},{10,1... | collective-permute-start | bytes 884744 | tf_op jit(solution)/shard_map/ppermute | solution.py:217
  230.3 8.6 %collective-permute-start.44 = (bf16[128,1152]{1,0:T(8,128)(2,1)S(1)}, bf16[128,1152]{1,0:T(8,128)(2,1)S(1)}, u32[]{:S(2)}, u32[]{:S(2)}) collective-permute-start(bf16[128,1152]{1,0:T(8,128)(2,1)S(1)} %get-tuple-element.306), channel_id=1, source_target_pairs={{0,3},{1,0},{2,1},{3,2},{4,7},{5,4},{6,5},{7,6},{8,11},{9,8},{10,9... | collective-permute-start | bytes 884744 | tf_op jit(solution)/shard_map/ppermute | solution.py:217
  266.8 9.0 %collective-permute-start.50 = (bf16[128,1152]{1,0:T(8,128)(2,1)}, bf16[128,1152]{1,0:T(8,128)(2,1)}, u32[]{:S(2)}, u32[]{:S(2)}) collective-permute-start(bf16[128,1152]{1,0:T(8,128)(2,1)} %pad_maximum_fusion.30), channel_id=1, source_target_pairs={{0,1},{1,2},{2,3},{3,0},{4,5},{5,6},{6,7},{7,4},{8,9},{9,10},{10,1... | collective-permute-start | bytes 884744 | tf_op jit(solution)/shard_map/ppermute | solution.py:217
  280.1 10.6 %collective-permute-start.53 = (bf16[128,1152]{1,0:T(8,128)(2,1)S(1)}, bf16[128,1152]{1,0:T(8,128)(2,1)S(1)}, u32[]{:S(2)}, u32[]{:S(2)}) collective-permute-start(bf16[128,1152]{1,0:T(8,128)(2,1)S(1)} %get-tuple-element.300), channel_id=1, source_target_pairs={{0,1},{1,2},{2,3},{3,0},{4,5},{5,6},{6,7},{7,4},{8,9},{9,10},{10,1... | collective-permute-start | bytes 884744 | tf_op jit(solution)/shard_map/ppermute | solution.py:217
  281.3 10.2 %collective-permute-start.54 = (bf16[128,1152]{1,0:T(8,128)(2,1)S(1)}, bf16[128,1152]{1,0:T(8,128)(2,1)S(1)}, u32[]{:S(2)}, u32[]{:S(2)}) collective-permute-start(bf16[128,1152]{1,0:T(8,128)(2,1)S(1)} %get-tuple-element.300), channel_id=1, source_target_pairs={{0,3},{1,0},{2,1},{3,2},{4,7},{5,4},{6,5},{7,6},{8,11},{9,8},{10,9... | collective-permute-start | bytes 884744 | tf_op jit(solution)/shard_map/ppermute | solution.py:217
  292.2 145.2 %reduce-scatter.6.cloned.1.call-start = ((), (), s32[]{:S(2)}) async-start(), calls=%async_computation.9 | async-start | bytes 3133440 | tf_op jit(solution)/shard_map/reduce_scatter | solution.py:377
  301.1 14.5 %collective-permute-start.58 = (bf16[128,1152]{1,0:T(8,128)(2,1)S(1)}, bf16[128,1152]{1,0:T(8,128)(2,1)S(1)}, u32[]{:S(2)}, u32[]{:S(2)}) collective-permute-start(bf16[128,1152]{1,0:T(8,128)(2,1)S(1)} %pad_maximum_fusion.32), channel_id=1, source_target_pairs={{0,1},{1,2},{2,3},{3,0},{4,5},{5,6},{6,7},{7,4},{8,9},{9,10},{10,1... | collective-permute-start | bytes 884744 | tf_op jit(solution)/shard_map/ppermute | solution.py:217
  301.8 13.8 %collective-permute-start.59 = (bf16[128,1152]{1,0:T(8,128)(2,1)S(1)}, bf16[128,1152]{1,0:T(8,128)(2,1)S(1)}, u32[]{:S(2)}, u32[]{:S(2)}) collective-permute-start(bf16[128,1152]{1,0:T(8,128)(2,1)S(1)} %pad_maximum_fusion.33), channel_id=1, source_target_pairs={{0,3},{1,0},{2,1},{3,2},{4,7},{5,4},{6,5},{7,6},{8,11},{9,8},{10,9... | collective-permute-start | bytes 884744 | tf_op jit(solution)/shard_map/ppermute | solution.py:217
  339.9 9.4 %collective-permute-start.63 = (bf16[128,1152]{1,0:T(8,128)(2,1)S(1)}, bf16[128,1152]{1,0:T(8,128)(2,1)S(1)}, u32[]{:S(2)}, u32[]{:S(2)}) collective-permute-start(bf16[128,1152]{1,0:T(8,128)(2,1)S(1)} %pad_maximum_fusion.34), channel_id=1, source_target_pairs={{0,1},{1,2},{2,3},{3,0},{4,5},{5,6},{6,7},{7,4},{8,9},{9,10},{10,1... | collective-permute-start | bytes 884744 | tf_op jit(solution)/shard_map/ppermute | solution.py:217
  341.4 8.0 %collective-permute-start.64 = (bf16[128,1152]{1,0:T(8,128)(2,1)S(1)}, bf16[128,1152]{1,0:T(8,128)(2,1)S(1)}, u32[]{:S(2)}, u32[]{:S(2)}) collective-permute-start(bf16[128,1152]{1,0:T(8,128)(2,1)S(1)} %pad_maximum_fusion.35), channel_id=1, source_target_pairs={{0,3},{1,0},{2,1},{3,2},{4,7},{5,4},{6,5},{7,6},{8,11},{9,8},{10,9... | collective-permute-start | bytes 884744 | tf_op jit(solution)/shard_map/ppermute | solution.py:217
  344.8 8.6 %collective-permute-start.67 = (bf16[4,144,1152]{2,1,0:T(8,128)(2,1)S(1)}, bf16[4,144,1152]{2,1,0:T(8,128)(2,1)S(1)}, u32[]{:S(2)}, u32[]{:S(2)}) collective-permute-start(bf16[4,144,1152]{2,1,0:T(8,128)(2,1)S(1)} %broadcast_select_fusion.5), channel_id=1, source_target_pairs={{0,16},{16,0},{1,17},{17,1},{2,18},{18,2},{3,19},{19,3},{4,20},{20... | collective-permute-start | bytes 3981320 | tf_op jit(solution)/shard_map/ppermute | solution.py:20
  350.1 8.6 %collective-permute-start.65 = (bf16[128,1152]{1,0:T(8,128)(2,1)S(1)}, bf16[128,1152]{1,0:T(8,128)(2,1)}, u32[]{:S(2)}, u32[]{:S(2)}) collective-permute-start(bf16[128,1152]{1,0:T(8,128)(2,1)S(1)} %get-tuple-element.284), channel_id=1, source_target_pairs={{0,1},{1,2},{2,3},{3,0},{4,5},{5,6},{6,7},{7,4},{8,9},{9,10},{10,1... | collective-permute-start | bytes 884744 | tf_op jit(solution)/shard_map/ppermute | solution.py:217
  351.1 7.7 %collective-permute-start.66 = (bf16[128,1152]{1,0:T(8,128)(2,1)S(1)}, bf16[128,1152]{1,0:T(8,128)(2,1)}, u32[]{:S(2)}, u32[]{:S(2)}) collective-permute-start(bf16[128,1152]{1,0:T(8,128)(2,1)S(1)} %get-tuple-element.284), channel_id=1, source_target_pairs={{0,3},{1,0},{2,1},{3,2},{4,7},{5,4},{6,5},{7,6},{8,11},{9,8},{10,9... | collective-permute-start | bytes 884744 | tf_op jit(solution)/shard_map/ppermute | solution.py:217
  374.7 7.6 %collective-permute-start.70 = (bf16[64,1152]{1,0:T(8,128)(2,1)S(1)}, bf16[64,1152]{1,0:T(8,128)(2,1)S(1)}, u32[]{:S(2)}, u32[]{:S(2)}) collective-permute-start(bf16[64,1152]{1,0:T(8,128)(2,1)S(1)} %get-tuple-element.346), channel_id=1, source_target_pairs={{0,1},{1,2},{2,3},{3,0},{4,5},{5,6},{6,7},{7,4},{8,9},{9,10},{10,1... | collective-permute-start | bytes 442376 | tf_op jit(solution)/shard_map/ppermute | solution.py:217
  383.1 8.0 %collective-permute-start.71 = (bf16[128,1152]{1,0:T(8,128)(2,1)S(1)}, bf16[128,1152]{1,0:T(8,128)(2,1)S(1)}, u32[]{:S(2)}, u32[]{:S(2)}) collective-permute-start(bf16[128,1152]{1,0:T(8,128)(2,1)S(1)} %pad_maximum_fusion.36), channel_id=1, source_target_pairs={{0,1},{1,2},{2,3},{3,0},{4,5},{5,6},{6,7},{7,4},{8,9},{9,10},{10,1... | collective-permute-start | bytes 884744 | tf_op jit(solution)/shard_map/ppermute | solution.py:217
  393.4 10.6 %collective-permute-start.74 = (bf16[128,1152]{1,0:T(8,128)(2,1)S(1)}, bf16[128,1152]{1,0:T(8,128)(2,1)S(1)}, u32[]{:S(2)}, u32[]{:S(2)}) collective-permute-start(bf16[128,1152]{1,0:T(8,128)(2,1)S(1)} %get-tuple-element.294), channel_id=1, source_target_pairs={{0,1},{1,2},{2,3},{3,0},{4,5},{5,6},{6,7},{7,4},{8,9},{9,10},{10,1... | collective-permute-start | bytes 884744 | tf_op jit(solution)/shard_map/ppermute | solution.py:217
  394.8 9.2 %collective-permute-start.75 = (bf16[128,1152]{1,0:T(8,128)(2,1)S(1)}, bf16[128,1152]{1,0:T(8,128)(2,1)S(1)}, u32[]{:S(2)}, u32[]{:S(2)}) collective-permute-start(bf16[128,1152]{1,0:T(8,128)(2,1)S(1)} %get-tuple-element.294), channel_id=1, source_target_pairs={{0,3},{1,0},{2,1},{3,2},{4,7},{5,4},{6,5},{7,6},{8,11},{9,8},{10,9... | collective-permute-start | bytes 884744 | tf_op jit(solution)/shard_map/ppermute | solution.py:217
  404.1 86.8 %reduce-scatter.8.cloned.1.call-start = ((), (), s32[]{:S(2)}) async-start(), calls=%async_computation.10 | async-start | bytes 1658880 | tf_op jit(solution)/shard_map/reduce_scatter | solution.py:498
  425.9 8.2 %collective-permute-start.79 = (bf16[2,512,512]{2,1,0:T(8,128)(2,1)}, bf16[2,512,512]{2,1,0:T(8,128)(2,1)}, u32[]{:S(2)}, u32[]{:S(2)}) collective-permute-start(bf16[2,512,512]{2,1,0:T(8,128)(2,1)} %get-tuple-element.187), channel_id=1, source_target_pairs={{0,16},{16,0},{1,17},{17,1},{2,18},{18,2},{3,19},{19,3},{4,20},{20... | collective-permute-start | bytes 3145736 | tf_op jit(solution)/shard_map/ppermute | solution.py:20
  441.3 28.8 %all-to-all-start.2 = ((bf16[8,272,288]{2,1,0:T(8,128)(2,1)}), bf16[8,272,288]{2,1,0:T(8,128)(2,1)}, u32[]{:S(2)}, u32[]{:S(2)}) async-start(bf16[8,272,288]{2,1,0:T(8,128)(2,1)} %shard_map.169), calls=%async_computation.4 | async-start | bytes 3342336 | tf_op jit(solution)/shard_map/all_to_all | solution.py:284
  451.6 7.5 %collective-permute-start.80 = (bf16[64,1152]{1,0:T(8,128)(2,1)S(1)}, bf16[64,1152]{1,0:T(8,128)(2,1)S(1)}, u32[]{:S(2)}, u32[]{:S(2)}) collective-permute-start(bf16[64,1152]{1,0:T(8,128)(2,1)S(1)} %get-tuple-element.343), channel_id=1, source_target_pairs={{0,1},{1,2},{2,3},{3,0},{4,5},{5,6},{6,7},{7,4},{8,9},{9,10},{10,1... | collective-permute-start | bytes 442376 | tf_op jit(solution)/shard_map/ppermute | solution.py:217
  459.3 9.9 %collective-permute-start.87 = (bf16[128,1152]{1,0:T(8,128)(2,1)S(1)}, bf16[128,1152]{1,0:T(8,128)(2,1)S(1)}, u32[]{:S(2)}, u32[]{:S(2)}) collective-permute-start(bf16[128,1152]{1,0:T(8,128)(2,1)S(1)} %pad_maximum_fusion.38), channel_id=1, source_target_pairs={{0,1},{1,2},{2,3},{3,0},{4,5},{5,6},{6,7},{7,4},{8,9},{9,10},{10,1... | collective-permute-start | bytes 884744 | tf_op jit(solution)/shard_map/ppermute | solution.py:217
  461.0 8.2 %collective-permute-start.88 = (bf16[128,1152]{1,0:T(8,128)(2,1)S(1)}, bf16[128,1152]{1,0:T(8,128)(2,1)S(1)}, u32[]{:S(2)}, u32[]{:S(2)}) collective-permute-start(bf16[128,1152]{1,0:T(8,128)(2,1)S(1)} %pad_maximum_fusion.39), channel_id=1, source_target_pairs={{0,3},{1,0},{2,1},{3,2},{4,7},{5,4},{6,5},{7,6},{8,11},{9,8},{10,9... | collective-permute-start | bytes 884744 | tf_op jit(solution)/shard_map/ppermute | solution.py:217
  482.0 8.7 %collective-permute-start.84 = (bf16[144,1152]{1,0:T(8,128)(2,1)S(1)}, bf16[144,1152]{1,0:T(8,128)(2,1)S(1)}, u32[]{:S(2)}, u32[]{:S(2)}) collective-permute-start(bf16[144,1152]{1,0:T(8,128)(2,1)S(1)} %pad_maximum_fusion.20), channel_id=1, source_target_pairs={{0,4},{4,8},{8,12},{12,0},{1,5},{5,9},{9,13},{13,1},{2,6},{6,10},{... | collective-permute-start | bytes 995336 | tf_op jit(solution)/shard_map/ppermute | solution.py:217
  482.4 8.3 %collective-permute-start.86 = (bf16[144,1152]{1,0:T(8,128)(2,1)S(1)}, bf16[144,1152]{1,0:T(8,128)(2,1)S(1)}, u32[]{:S(2)}, u32[]{:S(2)}) collective-permute-start(bf16[144,1152]{1,0:T(8,128)(2,1)S(1)} %pad_maximum_fusion.21), channel_id=1, source_target_pairs={{0,12},{4,0},{8,4},{12,8},{1,13},{5,1},{9,5},{13,9},{2,14},{6,2},{... | collective-permute-start | bytes 995336 | tf_op jit(solution)/shard_map/ppermute | solution.py:217
  493.1 18.1 %all-to-all-start.3 = ((bf16[8,144,288]{2,1,0:T(8,128)(2,1)}), bf16[8,144,288]{2,1,0:T(8,128)(2,1)S(1)}, u32[]{:S(2)}, u32[]{:S(2)}) async-start(bf16[8,144,288]{2,1,0:T(8,128)(2,1)} %shard_map.170), calls=%async_computation.6 | async-start | bytes 1769472 | tf_op jit(solution)/shard_map/all_to_all | solution.py:284
  503.8 19.0 %collective-permute-start.89 = (bf16[64,1152]{1,0:T(8,128)(2,1)S(1)}, bf16[64,1152]{1,0:T(8,128)(2,1)S(1)}, u32[]{:S(2)}, u32[]{:S(2)}) collective-permute-start(bf16[64,1152]{1,0:T(8,128)(2,1)S(1)} %copy-done.124), channel_id=1, source_target_pairs={{12,0},{8,4},{28,8},{24,12},{76,16},{72,20},{92,24},{88,28},{4,64}... | collective-permute-start | bytes 442376 | tf_op jit(solution)/shard_map/ppermute | solution.py:513
  506.8 16.1 %collective-permute-start.90 = (bf16[64,1152]{1,0:T(8,128)(2,1)S(1)}, bf16[64,1152]{1,0:T(8,128)(2,1)S(1)}, u32[]{:S(2)}, u32[]{:S(2)}) collective-permute-start(bf16[64,1152]{1,0:T(8,128)(2,1)S(1)} %get-tuple-element.203), channel_id=1, source_target_pairs={{8,0},{12,4},{24,8},{28,12},{72,16},{76,20},{88,24},{92,28},{0,64}... | collective-permute-start | bytes 442376 | tf_op jit(solution)/shard_map/ppermute | solution.py:513
  507.1 15.7 %collective-permute-start.91 = (bf16[64,1152]{1,0:T(8,128)(2,1)S(1)}, bf16[64,1152]{1,0:T(8,128)(2,1)S(1)}, u32[]{:S(2)}, u32[]{:S(2)}) collective-permute-start(bf16[64,1152]{1,0:T(8,128)(2,1)S(1)} %get-tuple-element.204), channel_id=1, source_target_pairs={{4,0},{0,4},{20,8},{16,12},{68,16},{64,20},{84,24},{80,28},{12,64}... | collective-permute-start | bytes 442376 | tf_op jit(solution)/shard_map/ppermute | solution.py:513
  507.6 15.2 %collective-permute-start.92 = (bf16[64,1152]{1,0:T(8,128)(2,1)S(1)}, bf16[64,1152]{1,0:T(8,128)(2,1)S(1)}, u32[]{:S(2)}, u32[]{:S(2)}) collective-permute-start(bf16[64,1152]{1,0:T(8,128)(2,1)S(1)} %get-tuple-element.205), channel_id=1, source_target_pairs={{0,0},{4,4},{16,8},{20,12},{64,16},{68,20},{80,24},{84,28},{8,64},... | collective-permute-start | bytes 442376 | tf_op jit(solution)/shard_map/ppermute | solution.py:513
  511.3 24.0 %all-to-all-start.4 = ((f32[128,8,128]{2,1,0:T(8,128)}), f32[128,8,128]{2,1,0:T(8,128)S(1)}, u32[]{:S(2)}, u32[]{:S(2)}) async-start(f32[128,8,128]{2,1,0:T(8,128)} %pad_maximum_fusion.17), calls=%async_computation.7 | async-start | bytes 1048576 | tf_op jit(solution)/shard_map/all_to_all | solution.py:528
  (221 other events, 1284.8 us)
Sparse Core Ops, SparseCore 0:
  48.1 30.3 all-gather.6
  84.0 35.8 all-gather.8
  127.4 44.1 all-gather.10
  292.3 32.2 reduce-scatter.3
  404.2 33.1 reduce-scatter.5
  439.6 24.3 reduce-scatter.7
